TPU v7x, 32 devices: a whole 2x2x4 slice. The times are simulated.
32 devices in a mesh: dp: 4 (over y, core), expert: 2 (over x), shard: 4 (over z).
Axes of the slice: x: 2, y: 2, z: 4, core: 2. Of those that a mesh axis runs over, the one named last changes fastest.
Arguments:
- tokens: bfloat16 [32768, 768], P(('dp', 'expert', 'shard')), may hold values from -6 to 6
- segments: int32 [32, 1024], P(('dp', 'expert', 'shard')), may hold values from 0 to 7, never falling along the last dimension, each value on 1 to 768 neighbouring positions
- routes: int32 [32768, 1], P(('dp', 'expert', 'shard')), may hold values from 0 to 3; in each aligned block of 1024 rows (0 to 1023, 1024 to 2047, ...) at most 512 rows name the same one
- cotangent: bfloat16 [32768, 768], P(('dp', 'expert', 'shard')), may hold values from -6 to 6
- attn_in: bfloat16 [768, 2304], P('shard'), may hold values from -0.21875 to 0.21875
- attn_out: bfloat16 [768, 768], P('shard'), may hold values from -1.75 to 1.75
- router: bfloat16 [768, 4], P('shard'), may hold values from -0.109375 to 0.109375
- gain_one: bfloat16 [768], P('shard'), may hold values from 0.5 to 1.5
- gain_two: bfloat16 [768], P('shard'), may hold values from 0.5 to 1.5
- expert_in: bfloat16 [4, 768, 3072], P('expert'), may hold values from -0.21875 to 0.21875
- expert_out: bfloat16 [4, 3072, 768], P('expert'), may hold values from -0.75 to 0.75
Outputs:
- layer_out: bfloat16 [32768, 768], P(('dp', 'expert', 'shard'))
- grad_tokens: bfloat16 [32768, 768], P(('dp', 'expert', 'shard'))
- grad_attn_in: float32 [768, 2304], P('shard')
- grad_attn_out: float32 [768, 768], P('shard')
- grad_router: float32 [768, 4], P('shard')
- grad_gain_one: float32 [768], P('shard')
- grad_gain_two: float32 [768], P('shard')
- grad_expert_in: float32 [4, 768, 3072], P('expert', None, 'shard')
- grad_expert_out: float32 [4, 3072, 768], P('expert', 'shard')
Inputs may be any that keep to these rules, and one draw needn't show every extreme that they name: `routes`: within the aligned blocks of 1024 token rows no expert is named by more than 512 rows, and in every draw some expert is named by exactly 512 rows of some block. `segments`: segment numbers never fall along a sequence; a document has at most 768 tokens, and some document has exactly that many.
All inputs are finite; a program needn't handle non-finite values.
Results may differ from a plain program's by a relative error of at most 0.022.
Values may be sent and summed in bfloat16 or wider, within the bound.
No kernel may reach another device: no remote copies, remote signals or barrier semaphores. Data moves between devices by JAX's collectives and lax.ppermute only.
A program may use at most 384 MiB of HBM per device.

v0:
```python
import math

import jax
import jax.numpy as jnp
from jax import lax
from jax.sharding import PartitionSpec as P

HEADS = 12
QBLOCK = 512


EPSILON = 1e-06
MASKED = -1e30


def rms_scale(values):
    return lax.rsqrt(jnp.mean(values * values, axis=-1, keepdims=True) + EPSILON)


def rms_backward(grad_norm, values, row_scale, gain_row):
    grad_gain = jnp.sum(grad_norm * values * row_scale, axis=0)
    scaled = grad_norm * gain_row
    scale_cubed = row_scale * row_scale * row_scale
    grad_values = row_scale * scaled - values * scale_cubed * jnp.mean(
        scaled * values, axis=-1, keepdims=True
    )
    return (grad_values, grad_gain)


def gelu_tanh(values):
    return jax.nn.gelu(values, approximate=True)


def split_heads(triple, head_count):
    length = triple.shape[0]
    head_dim = triple.shape[1] // (3 * head_count)
    parted = triple.reshape(length, 3, head_count, head_dim)
    return (parted[:, 0], parted[:, 1], parted[:, 2])


def block_scores(query_rows, key_rows, same_doc, inv_root):
    scores = (
        jnp.einsum("qhd,khd->hqk", query_rows, key_rows, preferred_element_type=jnp.float32)
        * inv_root
    )
    return jnp.where(same_doc[None], scores, MASKED)


def attend_forward(triple, seg_row, head_count, block_rows):
    query_all, key_all, value_all = split_heads(triple, head_count)
    length = triple.shape[0]
    inv_root = 1.0 / math.sqrt(query_all.shape[2])
    pieces = []
    kept_stats = []
    for row_start in range(0, length, block_rows):
        same_doc = seg_row[row_start : row_start + block_rows, None] == seg_row[None, :]
        scores = block_scores(
            query_all[row_start : row_start + block_rows], key_all, same_doc, inv_root
        )
        row_max = jnp.max(scores, axis=-1, keepdims=True)
        raised = jnp.exp(scores - row_max)
        row_total = jnp.sum(raised, axis=-1, keepdims=True)
        weights = (raised / row_total).astype(jnp.bfloat16)
        pieces.append(
            jnp.einsum("hqk,khd->qhd", weights, value_all, preferred_element_type=jnp.float32)
        )
        kept_stats.append((row_max, row_total))
    attended = jnp.concatenate(pieces, axis=0).reshape(length, -1).astype(jnp.bfloat16)
    return (attended, kept_stats)


def attend_backward(triple, seg_row, grad_out, kept_stats, head_count, block_rows):
    query_all, key_all, value_all = split_heads(triple, head_count)
    length = triple.shape[0]
    head_dim = query_all.shape[2]
    inv_root = 1.0 / math.sqrt(head_dim)
    grad_heads = grad_out.reshape(length, head_count, head_dim)
    grad_query = []
    grad_key = jnp.zeros(key_all.shape, jnp.float32)
    grad_value = jnp.zeros(value_all.shape, jnp.float32)
    for block_number, row_start in enumerate(range(0, length, block_rows)):
        same_doc = seg_row[row_start : row_start + block_rows, None] == seg_row[None, :]
        query_block = query_all[row_start : row_start + block_rows]
        grad_block = grad_heads[row_start : row_start + block_rows]
        scores = block_scores(query_block, key_all, same_doc, inv_root)
        row_max, row_total = kept_stats[block_number]
        probs_block = jnp.exp(scores - row_max) / row_total
        grad_probs = jnp.einsum(
            "qhd,khd->hqk", grad_block, value_all, preferred_element_type=jnp.float32
        )
        row_inner = jnp.sum(probs_block * grad_probs, axis=-1, keepdims=True)
        grad_scores = (probs_block * (grad_probs - row_inner)).astype(jnp.bfloat16)
        grad_query.append(
            jnp.einsum("hqk,khd->qhd", grad_scores, key_all, preferred_element_type=jnp.float32)
            * inv_root
        )
        grad_key = (
            grad_key
            + jnp.einsum(
                "hqk,qhd->khd", grad_scores, query_block, preferred_element_type=jnp.float32
            )
            * inv_root
        )
        grad_value = grad_value + jnp.einsum(
            "hqk,qhd->khd",
            probs_block.astype(jnp.bfloat16),
            grad_block,
            preferred_element_type=jnp.float32,
        )
    stacked = jnp.stack([jnp.concatenate(grad_query, axis=0), grad_key, grad_value], axis=1)
    return stacked.reshape(length, -1)


def regroup(partial_term, axis_dim, groups, shards):
    old_shape = partial_term.shape
    new_shape = (
        old_shape[:axis_dim]
        + (shards, groups, old_shape[axis_dim] // (shards * groups))
        + old_shape[axis_dim + 1 :]
    )
    swapped = jnp.swapaxes(partial_term.reshape(new_shape), axis_dim, axis_dim + 1)
    return swapped.reshape(old_shape)


def body(
    tokens,
    segments,
    routes,
    cotangent,
    attn_in,
    attn_out,
    router,
    gain_one,
    gain_two,
    expert_in,
    expert_out,
):
    full_in, full_out, full_router, full_gain_one, full_gain_two = (
        lax.all_gather(attn_in, "shard", axis=0, tiled=True),
        lax.all_gather(attn_out, "shard", axis=0, tiled=True),
        lax.all_gather(router, "shard", axis=0, tiled=True),
        lax.all_gather(gain_one, "shard", axis=0, tiled=True),
        lax.all_gather(gain_two, "shard", axis=0, tiled=True),
    )
    tok_rows, width = tokens.shape
    rows_all = tokens.astype(jnp.float32)
    first_gain = full_gain_one.astype(jnp.float32)
    second_gain = full_gain_two.astype(jnp.float32)
    scale_one = rms_scale(rows_all)
    normed = (rows_all * scale_one * first_gain).astype(jnp.bfloat16)
    triple = jnp.dot(normed, full_in, preferred_element_type=jnp.float32).astype(jnp.bfloat16)
    sequence = 0
    attended_seq, stats_seq = attend_forward(triple, segments[sequence], HEADS, QBLOCK)
    stats_all = [stats_seq]
    hidden_one = rows_all + jnp.dot(attended_seq, full_out, preferred_element_type=jnp.float32)
    scale_two = rms_scale(hidden_one)
    second = (hidden_one * scale_two * second_gain).astype(jnp.bfloat16)
    logits = jnp.dot(second, full_router, preferred_element_type=jnp.float32)
    router_probs = jax.nn.softmax(logits, axis=-1)
    experts_all = full_router.shape[1]
    exp_local = expert_in.shape[0]
    groups = lax.axis_size("expert")
    capacity = 2 * tok_rows // experts_all
    route_ids = routes[:, 0]
    choose = route_ids[:, None] == jnp.arange(experts_all, dtype=jnp.int32)[None, :]
    rank_inside = jnp.cumsum(choose.astype(jnp.int32), axis=0) - 1
    slot_index = route_ids * capacity + jnp.sum(jnp.where(choose, rank_inside, 0), axis=1)
    gate_value = jnp.sum(jnp.where(choose, router_probs, 0.0), axis=1)

    def to_slots(token_rows):
        filled = (
            jnp.zeros((experts_all * capacity, width), token_rows.dtype)
            .at[slot_index]
            .set(token_rows)
        )
        return filled.reshape(groups, exp_local, capacity, width)

    row_slots = to_slots(second)
    pre_act = jnp.einsum(
        "aecd,edf->aecf",
        lax.all_to_all(row_slots, "expert", split_axis=0, concat_axis=0, tiled=True),
        expert_in,
        preferred_element_type=jnp.float32,
    )
    activated = gelu_tanh(pre_act).astype(jnp.bfloat16)
    produced = jnp.einsum(
        "aecf,efd->aecd", activated, expert_out, preferred_element_type=jnp.float32
    ).astype(jnp.bfloat16)
    returned = lax.all_to_all(produced, "expert", split_axis=0, concat_axis=0, tiled=True)
    returned_rows = returned.reshape(experts_all * capacity, width)[slot_index]
    returned_wide = returned_rows.astype(jnp.float32)
    layer_out = (hidden_one + gate_value[:, None] * returned_wide).astype(jnp.bfloat16)
    grad_out = cotangent.astype(jnp.float32)
    grad_gate = jnp.sum(grad_out * returned_wide, axis=1)
    grad_slots = to_slots((gate_value[:, None] * grad_out).astype(jnp.bfloat16))
    grad_arrived, arrived = (
        lax.all_to_all(grad_slots, "expert", split_axis=0, concat_axis=0, tiled=True),
        lax.all_to_all(row_slots, "expert", split_axis=0, concat_axis=0, tiled=True),
    )
    pre_act = jnp.einsum("aecd,edf->aecf", arrived, expert_in, preferred_element_type=jnp.float32)
    activated = gelu_tanh(pre_act).astype(jnp.bfloat16)
    grad_expert_out = jnp.einsum(
        "aecf,aecd->efd", activated, grad_arrived, preferred_element_type=jnp.float32
    )
    grad_activated = jnp.einsum(
        "aecd,efd->aecf", grad_arrived, expert_out, preferred_element_type=jnp.float32
    )
    gelu_pull = jax.vjp(gelu_tanh, pre_act)[1]
    grad_pre = gelu_pull(grad_activated)[0].astype(jnp.bfloat16)
    grad_expert_in = jnp.einsum(
        "aecd,aecf->edf", arrived, grad_pre, preferred_element_type=jnp.float32
    )
    grad_expert_rows = jnp.einsum(
        "aecf,edf->aecd", grad_pre, expert_in, preferred_element_type=jnp.float32
    ).astype(jnp.bfloat16)
    grad_back = lax.all_to_all(grad_expert_rows, "expert", split_axis=0, concat_axis=0, tiled=True)
    grad_from_experts = grad_back.reshape(experts_all * capacity, width)[slot_index].astype(
        jnp.float32
    )
    grad_logits = (
        router_probs
        * (jnp.where(choose, grad_gate[:, None], 0.0) - (gate_value * grad_gate)[:, None])
    ).astype(jnp.bfloat16)
    grad_router_w = jnp.einsum("td,te->de", second, grad_logits, preferred_element_type=jnp.float32)
    grad_second = grad_from_experts + jnp.einsum(
        "te,de->td", grad_logits, full_router, preferred_element_type=jnp.float32
    )
    grad_hidden_two, grad_gain_two = rms_backward(grad_second, hidden_one, scale_two, second_gain)
    grad_hidden = grad_out + grad_hidden_two
    grad_branch = grad_hidden.astype(jnp.bfloat16)
    grad_attn_out_w = jnp.einsum(
        "td,te->de", attended_seq, grad_branch, preferred_element_type=jnp.float32
    )
    grad_attended = jnp.einsum(
        "te,de->td", grad_branch, full_out, preferred_element_type=jnp.float32
    ).astype(jnp.bfloat16)
    sequence = 0
    grad_parts = attend_backward(
        triple, segments[sequence], grad_attended, stats_all[sequence], HEADS, QBLOCK
    )
    grad_triple = grad_parts.astype(jnp.bfloat16)
    grad_attn_in_w = jnp.einsum(
        "td,te->de", normed, grad_triple, preferred_element_type=jnp.float32
    )
    grad_normed = jnp.einsum("te,de->td", grad_triple, full_in, preferred_element_type=jnp.float32)
    grad_rows_one, grad_gain_one = rms_backward(grad_normed, rows_all, scale_one, first_gain)
    grad_tokens = (grad_hidden + grad_rows_one).astype(jnp.bfloat16)
    attn_parts = (
        lax.psum_scatter(
            grad_attn_in_w.astype(jnp.bfloat16), "shard", scatter_dimension=0, tiled=True
        ).astype(jnp.float32),
        lax.psum_scatter(
            grad_attn_out_w.astype(jnp.bfloat16), "shard", scatter_dimension=0, tiled=True
        ).astype(jnp.float32),
        lax.psum_scatter(
            grad_router_w.astype(jnp.bfloat16), "shard", scatter_dimension=0, tiled=True
        ).astype(jnp.float32),
        lax.psum_scatter(
            grad_gain_one.astype(jnp.bfloat16), "shard", scatter_dimension=0, tiled=True
        ).astype(jnp.float32),
        lax.psum_scatter(
            grad_gain_two.astype(jnp.bfloat16), "shard", scatter_dimension=0, tiled=True
        ).astype(jnp.float32),
    )
    attn_total = (
        lax.psum(attn_parts[0].astype(jnp.bfloat16), ("dp", "expert")).astype(jnp.float32),
        lax.psum(attn_parts[1].astype(jnp.bfloat16), ("dp", "expert")).astype(jnp.float32),
        lax.psum(attn_parts[2].astype(jnp.bfloat16), ("dp", "expert")).astype(jnp.float32),
        lax.psum(attn_parts[3].astype(jnp.bfloat16), ("dp", "expert")).astype(jnp.float32),
        lax.psum(attn_parts[4].astype(jnp.bfloat16), ("dp", "expert")).astype(jnp.float32),
    )
    data_groups = lax.axis_size("dp")
    shard_count = lax.axis_size("shard")
    spread_in = regroup(grad_expert_in, 2, data_groups, shard_count)
    spread_out = regroup(grad_expert_out, 1, data_groups, shard_count)
    summed_in, summed_out = (
        lax.psum_scatter(
            spread_in.astype(jnp.bfloat16), ("dp", "shard"), scatter_dimension=2, tiled=True
        ).astype(jnp.float32),
        lax.psum_scatter(
            spread_out.astype(jnp.bfloat16), ("dp", "shard"), scatter_dimension=1, tiled=True
        ).astype(jnp.float32),
    )
    final_in, final_out = (
        lax.all_gather(summed_in.astype(jnp.bfloat16), "dp", axis=2, tiled=True).astype(
            summed_in.dtype
        ),
        lax.all_gather(summed_out.astype(jnp.bfloat16), "dp", axis=1, tiled=True).astype(
            summed_out.dtype
        ),
    )
    return (
        layer_out,
        grad_tokens,
        attn_total[0],
        attn_total[1],
        attn_total[2],
        attn_total[3],
        attn_total[4],
        final_in,
        final_out,
    )


def solution(mesh):
    placed = (
        P(("dp", "expert", "shard"), None),
        P(("dp", "expert", "shard"), None),
        P(("dp", "expert", "shard"), None),
        P(("dp", "expert", "shard"), None),
        P("shard", None),
        P("shard", None),
        P("shard", None),
        P("shard"),
        P("shard"),
        P("expert", None, None),
        P("expert", None, None),
    )
    return jax.shard_map(
        body,
        mesh=mesh,
        in_specs=placed,
        out_specs=(
            P(("dp", "expert", "shard"), None),
            P(("dp", "expert", "shard"), None),
            P("shard", None),
            P("shard", None),
            P("shard", None),
            P("shard"),
            P("shard"),
            P("expert", None, "shard"),
            P("expert", "shard", None),
        ),
        check_vma=False,
    )
```

profile of v0, /device:TPU:1, one launch (start us, length us, event | category | flops | bytes accessed | tf_op | source)
XLA Modules:
  0.0 1085.3 jit_solution(14301247567798198982)
XLA Ops:
  31.1 50.6 %all-gather.6.cloned.1.call-done = bf16[768,2304]{1,0:T(8,128)(2,1)} async-done(((bf16[192,2304]{1,0:T(8,128)(2,1)}), bf16[768,2304]{1,0:T(8,128)(2,1)}) %all-gather.6.cloned.1.call-update) | async-done | bytes 3538960 | tf_op jit(solution)/shard_map/all_gather | solution.py:139
  119.8 33.1 %fusion.112 = (f32[12,512]{1,0:T(8,128)S(1)}, f32[12,512,1024]{2,1,0:T(8,128)}) fusion(f32[12,512,1024]{2,1,0:T(8,128)} %fusion.90, pred[512,1024]{1,0:T(8,128)(4,1)S(1)} %get-tuple-element.62), kind=kOutput, calls=%fused_computation.159 | output fusion | flops 37749760 | bytes 50880512 | tf_op jit(solution)/shard_map/sub | solution.py:61
  164.6 33.0 %fusion.113 = (f32[12,512]{1,0:T(8,128)S(1)}, f32[12,512,1024]{2,1,0:T(8,128)}) fusion(f32[12,512,1024]{2,1,0:T(8,128)} %fusion.91, pred[512,1024]{1,0:T(8,128)(4,1)S(1)} %get-tuple-element.61), kind=kOutput, calls=%fused_computation.160 | output fusion | flops 37749760 | bytes 50880512 | tf_op jit(solution)/shard_map/sub | solution.py:61
  223.0 39.7 %all_to_all.21 = bf16[2,2,512,768]{3,2,1,0:T(8,128)(2,1)S(1)} all-to-all(bf16[2,2,512,768]{3,2,1,0:T(8,128)(2,1)} %bitcast.188), channel_id=1, replica_groups=mesh['dp'=4,'expert'=2,'shard'=4] {'expert'}, dimensions={0} | all-to-all | bytes 6291456 | tf_op jit(solution)/shard_map/all_to_all | solution.py:181
  264.5 16.9 %fusion.25 = f32[2,2,512,3072]{3,2,1,0:T(8,128)} fusion(bf16[2,768,3072]{2,1,0:T(8,128)(2,1)} %param.20, bf16[2,2,512,768]{3,2,1,0:T(8,128)(2,1)S(1)} %all_to_all.21), kind=kOutput, calls=%fused_computation.46 | convolution fusion | flops 9663676416 | bytes 37748736 | tf_op jit(solution)/shard_map/aecd,edf->aecf/dot_general | solution.py:179
  281.4 18.8 %convert_bitcast_fusion.1 = bf16[2,2,512,768]{3,2,0,1:T(8,128)(2,1)S(1)} fusion(bf16[2,3072,768]{2,1,0:T(8,128)(2,1)} %param.21, f32[2,2,512,3072]{3,2,1,0:T(8,128)} %fusion.25), kind=kOutput, calls=%fused_computation.94 | convolution fusion | flops 9721872384 | bytes 37748736 | tf_op jit(solution)/shard_map/aecf,efd->aecd/dot_general | solution.py:186
  320.4 20.2 %all-to-all-done.1 = bf16[2,2,512,768]{3,2,1,0:T(8,128)(2,1)S(1)} async-done(((bf16[2,2,512,768]{3,2,1,0:T(8,128)(2,1)}), bf16[2,2,512,768]{3,2,1,0:T(8,128)(2,1)S(1)}, u32[]{:S(2)}, u32[]{:S(2)}) %all-to-all-start.1) | async-done | bytes 3145760 | tf_op jit(solution)/shard_map/all_to_all | solution.py:189
  358.7 37.6 %all_to_all.22 = bf16[2,2,512,768]{3,2,1,0:T(8,128)(2,1)S(1)} all-to-all(bf16[2,2,512,768]{3,2,1,0:T(8,128)(2,1)} %bitcast.187), channel_id=1, replica_groups=mesh['dp'=4,'expert'=2,'shard'=4] {'expert'}, dimensions={0} | all-to-all | bytes 6291456 | tf_op jit(solution)/shard_map/all_to_all | solution.py:197
  396.3 29.2 %fusion.8 = bf16[2,2,512,3072]{3,2,0,1:T(8,128)(2,1)} fusion(f32[2,2,512,3072]{3,2,1,0:T(8,128)} %fusion.25, bf16[2,3072,768]{2,1,0:T(8,128)(2,1)} %param.21, bf16[2,2,512,768]{3,2,1,0:T(8,128)(2,1)S(1)} %all_to_all.22), kind=kOutput, calls=%fused_computation.14 | convolution fusion | flops 9789505536 | bytes 50331648 | tf_op jit(solution)/shard_map/aecd,efd->aecf/dot_general | solution.py:205
  425.6 15.7 %convert_bitcast_fusion = bf16[2,2,512,768]{3,2,0,1:T(8,128)(2,1)S(1)} fusion(bf16[2,2,512,3072]{3,2,0,1:T(8,128)(2,1)} %fusion.8, bf16[2,768,3072]{2,1,0:T(8,128)(2,1)} %param.20), kind=kOutput, calls=%fused_computation.93 | convolution fusion | flops 9665249280 | bytes 25165824 | tf_op jit(solution)/shard_map/aecf,edf->aecd/dot_general | solution.py:213
  447.2 32.5 %all-to-all-done.3 = bf16[2,2,512,768]{3,2,1,0:T(8,128)(2,1)S(1)} async-done(((bf16[2,2,512,768]{3,2,1,0:T(8,128)(2,1)}), bf16[2,2,512,768]{3,2,1,0:T(8,128)(2,1)S(1)}, u32[]{:S(2)}, u32[]{:S(2)}) %all-to-all-start.3) | async-done | bytes 3145760 | tf_op jit(solution)/shard_map/all_to_all | solution.py:216
  513.2 17.4 %multiply_reduce_fusion = (f32[12,512]{1,0:T(8,128)S(1)}, f32[12,512,1024]{2,1,0:T(8,128)}) fusion(f32[12,512,1024]{2,1,0:T(8,128)} %get-tuple-element.68, f32[12,512]{1,0:T(8,128)S(1)} %copy-done.24, bf16[512,12,64]{0,2,1:T(8,128)(2,1)S(1)} %bitcast.197, bf16[1024,3,12,64]{0,3,2,1:T(8,128)(2,1)} %bitcast.177), kind=kOutput, calls=%fused_computation.23 | convolution fusion | flops 824174592 | bytes 52740096 | tf_op jit(solution)/shard_map/qhd,khd->hqk/dot_general | solution.py:88
  530.7 18.0 %multiply_reduce_fusion.1 = (f32[12,512]{1,0:T(8,128)S(1)}, f32[12,512,1024]{2,1,0:T(8,128)}) fusion(f32[12,512,1024]{2,1,0:T(8,128)} %get-tuple-element.70, f32[12,512]{1,0:T(8,128)S(1)} %copy-done.26, bf16[512,12,64]{0,2,1:T(8,128)(2,1)S(1)} %bitcast.194, bf16[1024,3,12,64]{0,3,2,1:T(8,128)(2,1)} %bitcast.178), kind=kOutput, calls=%fused_computation.25 | convolution fusion | flops 824174592 | bytes 52740096 | tf_op jit(solution)/shard_map/qhd,khd->hqk/dot_general | solution.py:88
  560.8 21.2 %multiply_convert_fusion.1 = bf16[12,512,1024]{2,1,0:T(8,128)(2,1)} fusion(f32[12,512,1024]{2,1,0:T(8,128)} %get-tuple-element.77, f32[12,512]{1,0:T(8,128)S(1)} %get-tuple-element.76, f32[12,512,1024]{2,1,0:T(8,128)} %get-tuple-element.70, f32[12,512]{1,0:T(8,128)S(1)} %copy-done.26), kind=kLoop, calls=%fused_computation.24 | loop fusion | flops 25165824 | bytes 62963712 | tf_op jit(solution)/shard_map/convert_element_type | solution.py:92
  591.0 21.4 %multiply_convert_fusion = bf16[12,512,1024]{2,1,0:T(8,128)(2,1)} fusion(f32[12,512,1024]{2,1,0:T(8,128)} %get-tuple-element.79, f32[12,512]{1,0:T(8,128)S(1)} %get-tuple-element.78, f32[12,512,1024]{2,1,0:T(8,128)} %get-tuple-element.68, f32[12,512]{1,0:T(8,128)S(1)} %copy-done.24), kind=kLoop, calls=%fused_computation.22 | loop fusion | flops 25165824 | bytes 62963712 | tf_op jit(solution)/shard_map/convert_element_type | solution.py:92
  641.2 24.2 %bitcast_convert_fusion = bf16[2,3072,768]{2,1,0:T(8,128)(2,1)} fusion(bf16[2,2,512,768]{3,2,1,0:T(8,128)(2,1)} %copy-done.15, f32[2,2,512,3072]{3,2,1,0:T(8,128)} %fusion.25), kind=kOutput, calls=%fused_computation.32 | convolution fusion | flops 9725018112 | bytes 37748736 | tf_op jit(solution)/shard_map/aecf,aecd->efd/dot_general | solution.py:202
  673.9 18.0 %bitcast_convert_fusion.1 = bf16[2,768,3072]{2,1,0:T(8,128)(2,1)} fusion(bf16[2,2,512,768]{3,2,1,0:T(8,128)(2,1)} %copy-done.14, bf16[2,2,512,3072]{3,2,0,1:T(8,128)(2,1)} %fusion.8), kind=kOutput, calls=%fused_computation.33 | convolution fusion | flops 9668395008 | bytes 25165824 | tf_op jit(solution)/shard_map/aecd,aecf->edf/dot_general | solution.py:210
  716.6 109.3 %reduce-scatter.14.cloned.1.call-done = bf16[2,192,768]{2,1,0:T(8,128)(2,1)} async-done(((bf16[2,3072,768]{2,1,0:T(8,128)(2,1)}), bf16[2,192,768]{2,1,0:T(8,128)(2,1)}) %reduce-scatter.14.cloned.1.call-update) | async-done | bytes 589840 | tf_op jit(solution)/shard_map/reduce_scatter | solution.py:280
  825.9 115.6 %reduce-scatter.12.cloned.1.call-done = bf16[2,768,192]{1,2,0:T(8,128)(2,1)} async-done(((bf16[2,768,3072]{1,2,0:T(8,128)(2,1)}), bf16[2,768,192]{1,2,0:T(8,128)(2,1)}) %reduce-scatter.12.cloned.1.call-update) | async-done | bytes 589840 | tf_op jit(solution)/shard_map/reduce_scatter | solution.py:277
  942.2 19.2 %reduce-scatter.16.cloned.1.call-done = bf16[192,4]{1,0:T(8,128)(2,1)} async-done(((bf16[768,4]{1,0:T(8,128)(2,1)}), bf16[192,4]{1,0:T(8,128)(2,1)}) %reduce-scatter.16.cloned.1.call-update) | async-done | bytes 1552
  980.5 17.4 %all-reduce.4 = (bf16[192,4]{0,1:T(4,128)(2,1)S(1)}, bf16[192]{0:T(256)(128)(2,1)S(1)}, bf16[192]{0:T(256)(128)(2,1)S(1)}) all-reduce(bf16[192,4]{0,1:T(4,128)(2,1)S(1)} %copy.93, bf16[192]{0:T(256)(128)(2,1)S(1)} %dynamic-slice.3, bf16[192]{0:T(256)(128)(2,1)S(1)} %dynamic-slice.5), channel_id=1, replica_groups=mesh['dp'=4,'expert'=2,'shard'=4] {'dp','expert'}, use_global_device_ids=true, to_apply=%region_24.25 | all-reduce | flops 1152 | bytes 4608 | tf_op jit(solution)/shard_map/psum | solution.py:268
  1004.9 16.8 %all-reduce.10.cloned.1.call-done = (bf16[192,2304]{1,0:T(8,128)(2,1)}, bf16[192,768]{1,0:T(8,128)(2,1)}) async-done(((bf16[192,2304]{1,0:T(8,128)(2,1)}, bf16[192,768]{1,0:T(8,128)(2,1)}), (bf16[192,2304]{1,0:T(8,128)(2,1)}, bf16[192,768]{1,0:T(8,128)(2,1)})) %all-reduce.10.cloned.1.call-update) | async-done | bytes 1179664 | tf_op jit(solution)/shard_map/psum | solution.py:266
  1026.0 21.9 %all-gather.12.cloned.1.call-done = bf16[2,768,768]{2,1,0:T(8,128)(2,1)} async-done(((bf16[2,192,768]{2,1,0:T(8,128)(2,1)}), bf16[2,768,768]{2,1,0:T(8,128)(2,1)}) %all-gather.12.cloned.1.call-update) | async-done | bytes 2359312 | tf_op jit(solution)/shard_map/all_gather | solution.py:288
  1052.1 21.3 %all-gather.10.cloned.1.call-done = bf16[2,768,768]{1,2,0:T(8,128)(2,1)} async-done(((bf16[2,768,192]{1,2,0:T(8,128)(2,1)}), bf16[2,768,768]{1,2,0:T(8,128)(2,1)}) %all-gather.10.cloned.1.call-update) | async-done | bytes 2359312 | tf_op jit(solution)/shard_map/all_gather | solution.py:285
  (191 shorter events, 299.8 us)
Async XLA Ops:
  7.2 23.3 %copy-start.30 = (s32[1,1024]{1,0:T(1,128)S(1)}, s32[1,1024]{1,0:T(1,128)}, u32[]{:S(2)}) copy-start(s32[1,1024]{1,0:T(1,128)} %param.12) | copy-start | bytes 12292
  7.2 74.5 %all-gather.6.cloned.1.call-start = ((), (), s32[]{:S(2)}) async-start(), calls=%async_computation.9 | async-start | bytes 4423680 | tf_op jit(solution)/shard_map/all_gather | solution.py:139
  7.9 201.5 %all-gather.8.cloned.1.call-start = ((), (), s32[]{:S(2)}) async-start(), calls=%async_computation.10 | async-start | bytes 1474560 | tf_op jit(solution)/shard_map/all_gather | solution.py:140
  23.2 66.3 %copy-start.31 = (f32[768]{0:T(1024)}, f32[768]{0:T(1024)S(1)}, u32[]{:S(2)}) copy-start(f32[768]{0:T(1024)S(1)} %convert_element_type.166) | copy-start | bytes 9220
  29.4 180.1 %copy-start.5 = (bf16[1024,768]{0,1:T(8,128)(2,1)}, bf16[1024,768]{0,1:T(8,128)(2,1)S(1)}, u32[]{:S(2)}) copy-start(bf16[1024,768]{0,1:T(8,128)(2,1)S(1)} %copy.60) | copy-start | bytes 4718596
  30.4 59.0 %copy-start.28 = (f32[1024]{0:T(1024)}, f32[1024]{0:T(1024)S(1)}, u32[]{:S(2)}) copy-start(f32[1024]{0:T(1024)S(1)} %get-tuple-element.58) | copy-start | bytes 12292
  302.1 38.5 %all-to-all-start.1 = ((bf16[2,2,512,768]{3,2,1,0:T(8,128)(2,1)}), bf16[2,2,512,768]{3,2,1,0:T(8,128)(2,1)S(1)}, u32[]{:S(2)}, u32[]{:S(2)}) async-start(bf16[2,2,512,768]{3,2,1,0:T(8,128)(2,1)} %copy.65), calls=%async_computation.1 | async-start | bytes 6291456 | tf_op jit(solution)/shard_map/all_to_all | solution.py:189
  306.2 14.2 %copy-start.20 = (s32[1024,1]{0,1:T(1,128)S(1)}, s32[1024,1]{0,1:T(1,128)}, u32[]{:S(2)}) copy-start(s32[1024,1]{0,1:T(1,128)} %param.13) | copy-start | bytes 12292
  396.3 29.2 %copy-start.15 = (bf16[2,2,512,768]{3,2,1,0:T(8,128)(2,1)}, bf16[2,2,512,768]{3,2,1,0:T(8,128)(2,1)S(1)}, u32[]{:S(2)}) copy-start(bf16[2,2,512,768]{3,2,1,0:T(8,128)(2,1)S(1)} %all_to_all.22) | copy-start | bytes 9437188
  443.1 36.5 %all-to-all-start.3 = ((bf16[2,2,512,768]{3,2,1,0:T(8,128)(2,1)}), bf16[2,2,512,768]{3,2,1,0:T(8,128)(2,1)S(1)}, u32[]{:S(2)}, u32[]{:S(2)}) async-start(bf16[2,2,512,768]{3,2,1,0:T(8,128)(2,1)} %copy.70), calls=%async_computation.3 | async-start | bytes 6291456 | tf_op jit(solution)/shard_map/all_to_all | solution.py:216
  447.1 268.7 %reduce-scatter.10.cloned.1.call-start = ((), (), s32[]{:S(2)}) async-start(), calls=%async_computation.12 | async-start | bytes 1474560 | tf_op jit(solution)/shard_map/reduce_scatter | solution.py:252
  447.2 40.7 %copy-start.21 = (bf16[1024,4]{0,1:T(4,128)(2,1)}, bf16[1024,4]{0,1:T(4,128)(2,1)S(1)}, u32[]{:S(2)}) copy-start(bf16[1024,4]{0,1:T(4,128)(2,1)S(1)} %multiply_convert_fusion.6) | copy-start | bytes 24580
  513.2 17.5 %copy-start.26 = (f32[12,512]{1,0:T(8,128)S(1)}, f32[12,512]{1,0:T(8,128)}, u32[]{:S(2)}) copy-start(f32[12,512]{1,0:T(8,128)} %copy-done.25) | copy-start | bytes 73732
  530.7 185.2 %reduce-scatter.8.cloned.1.call-start = ((), (), s32[]{:S(2)}) async-start(), calls=%async_computation.11 | async-start | bytes 4423680 | tf_op jit(solution)/shard_map/reduce_scatter | solution.py:249
  612.4 16.6 %slice-start = ((s8[12582912]{0:T(1024)(128)(4,1)}), s8[4194304]{0:T(1024)(128)(4,1)S(1)}, s32[]{:S(2)}) async-start(s8[12582912]{0:T(1024)(128)(4,1)} %bitcast.170), calls=%async_computation.19 | async-start | bytes 8388608
  612.4 16.6 %slice-start.1 = ((s8[12582912]{0:T(1024)(128)(4,1)}), s8[4194304]{0:T(1024)(128)(4,1)S(1)}, s32[]{:S(2)}) async-start(s8[12582912]{0:T(1024)(128)(4,1)} %bitcast.170), calls=%async_computation.20 | async-start | bytes 8388608
  641.1 184.7 %reduce-scatter.14.cloned.1.call-start = ((), (), s32[]{:S(2)}) async-start(), calls=%async_computation.15 | async-start | bytes 10027008 | tf_op jit(solution)/shard_map/reduce_scatter | solution.py:280
  673.8 267.7 %reduce-scatter.12.cloned.1.call-start = ((), (), s32[]{:S(2)}) async-start(), calls=%async_computation.13 | async-start | bytes 10027008 | tf_op jit(solution)/shard_map/reduce_scatter | solution.py:277
  713.0 248.4 %reduce-scatter.16.cloned.1.call-start = ((), (), s32[]{:S(2)}) async-start(), calls=%async_computation.17 | async-start | bytes 245760
  714.9 247.4 %copy-start.12 = (bf16[1024,768]{0,1:T(8,128)(2,1)S(1)}, bf16[1024,768]{0,1:T(8,128)(2,1)}, u32[]{:S(2)}) copy-start(bf16[1024,768]{0,1:T(8,128)(2,1)} %get-tuple-element.52) | copy-start | bytes 4718596
  715.8 305.9 %all-reduce.10.cloned.1.call-start = ((), (), s32[]{:S(2)}) async-start(), calls=%async_computation.18 | async-start | bytes 2359296 | tf_op jit(solution)/shard_map/psum | solution.py:266
  716.5 331.4 %all-gather.12.cloned.1.call-start = ((), (), s32[]{:S(2)}) async-start(), calls=%async_computation.16 | async-start | bytes 2949120 | tf_op jit(solution)/shard_map/all_gather | solution.py:288
  825.9 247.5 %all-gather.10.cloned.1.call-start = ((), (), s32[]{:S(2)}) async-start(), calls=%async_computation.14 | async-start | bytes 2949120 | tf_op jit(solution)/shard_map/all_gather | solution.py:285
  963.8 35.8 %copy-start.27 = (f32[1024]{0:T(1024)S(1)}, f32[1024]{0:T(1024)}, u32[]{:S(2)}) copy-start(f32[1024]{0:T(1024)} %get-tuple-element.57) | copy-start | bytes 12292
  (27 other events, 114.0 us)
Sparse Core Ops, SparseCore 0:
  9.6 72.0 all-gather.5
  83.3 28.4 all-gather.7
  530.8 31.6 reduce-scatter.9
  641.3 68.8 reduce-scatter.7
  714.1 111.7 reduce-scatter.13
  830.4 111.1 reduce-scatter.11
  944.3 16.9 reduce-scatter.15
  964.9 56.7 all-reduce.9
  1023.2 24.6 all-gather.11
  1049.3 24.0 all-gather.9
where the time goes:
time: 1090 us
  waiting for transfers between devices  410 us (38%)
  matrix products  294 us (27%)
  other arithmetic  134 us (12%)
  blocking collectives  123 us (11%)
  local copies, waits for them, and re-layouts  100 us (9%)
  between operations  16.5 us (2%)
    reduce_scatter x1, waiting for transfers between devices, body(): lax.psum_scatter(spread_in.astype(jnp.bfloat16), ('dp', 'shard'), scatter...  116 us
    reduce_scatter x1, waiting for transfers between devices, body(): lax.psum_scatter(spread_out.astype(jnp.bfloat16), ('dp', 'shard'), scatte...  109 us
    sub x2, other arithmetic, attend_forward(): raised = jnp.exp(scores - row_max)  66 us
    all_gather x1, waiting for transfers between devices, body(): lax.all_gather(attn_in, 'shard', axis=0, tiled=True)  50.6 us
    convert_element_type x2, other arithmetic, attend_backward(): grad_scores = (probs_block * (grad_probs - row_inner)).astype(jnp.bfloat16)  42.6 us
    all_to_all x1, blocking collectives, body(): lax.all_to_all(row_slots, 'expert', split_axis=0, concat_axis=0, tiled=True)  39.7 us
    all_to_all x1, blocking collectives, body(): lax.all_to_all(grad_slots, 'expert', split_axis=0, concat_axis=0, tiled=T...  37.6 us
    dot_general x2, matrix products, attend_backward(): jnp.einsum('qhd,khd->hqk', grad_block, value_all, preferred_element_type=...  35.4 us
  transfers between devices with their start and end apart: 12, of which 9 were waited for; matrix products, arithmetic and copies ran while one was open for 32% of the time, Pallas kernels for 0%

commit v1 on v0

v1 whole, which is shorter than its diff:
```python
import functools
import math

import jax
import jax.numpy as jnp
from jax import lax
from jax.experimental import pallas as pl
from jax.experimental.pallas import tpu as pltpu
from jax.sharding import PartitionSpec as P

HEADS = 12
LANES = 128
EPSILON = 1e-06
MASKED = -1e30
BF16 = jnp.bfloat16
F32 = jnp.float32
NN = (((1,), (0,)), ((), ()))
NT = (((1,), (1,)), ((), ()))
TN = (((0,), (0,)), ((), ()))
CHUNKS = 2
GROUPS = 3
GATHERS = 2
SHARE = 0.12
GELU_C = math.sqrt(2.0 / math.pi)
GELU_A = 0.044715


def dot(left, right, dims=NN):
    return lax.dot_general(left, right, dims, preferred_element_type=F32)


def params(mebibytes=60):
    return pltpu.CompilerParams(vmem_limit_bytes=mebibytes << 20)


def lasting(microseconds):
    return pl.CostEstimate(
        flops=int(microseconds * SHARE * 1.15e9), bytes_accessed=0, transcendentals=0
    )


def whole_spec(shape, buffers=1):
    return pl.BlockSpec(
        shape, lambda *_: (0,) * len(shape), pipeline_mode=pl.Buffered(buffers)
    )


def lane_parts(value, lane):
    high = value.astype(BF16).astype(F32)
    middle = (value - high).astype(BF16).astype(F32)
    low = value - high - middle
    return jnp.where(lane < 16, high, jnp.where(lane < 32, middle, low))


def attend_kernel(q_ref, k_ref, v_ref, segq_ref, segk_ref, out_ref, qaug_ref, lse_ref, *, block):
    pair, pairs = pl.program_id(0), pl.num_programs(0)
    rows, keys = q_ref.shape[0], k_ref.shape[0]
    lane_k = lax.broadcasted_iota(jnp.int32, (keys, LANES), 1)
    lane_q = lax.broadcasted_iota(jnp.int32, (rows, LANES), 1)
    k_mark = jnp.where((lane_k - 48) == segk_ref[...], 1.0, 0.0).astype(BF16)
    zone = (lane_q >= 48) & (lane_q < 56)
    q_mark = jnp.where(zone & ((lane_q - 48) != segq_ref[...]), MASKED, 0.0)

    @pl.when(pair == 0)
    def _():
        lse_ref[...] = jnp.zeros_like(lse_ref)

    k_mark = jnp.where((lane_k >= 48) & (lane_k < 56), k_mark, jnp.asarray(0, BF16))
    k_wide = jnp.concatenate([k_ref[...], k_mark], axis=1)
    v_wide = jnp.concatenate([v_ref[...], jnp.ones((keys, LANES), BF16)], axis=1)
    lane = lane_q[:block]
    for start in range(0, rows, block):
        part = slice(start, start + block)
        query = q_ref[part] * jnp.asarray(0.125, BF16)
        outs = []
        stats = lse_ref[part]
        for side in range(2):
            own = (lane >= 64) if side else (lane < 64)
            picked = jnp.where(own, query, jnp.asarray(0, BF16))
            scores = dot(
                jnp.concatenate([picked, q_mark[part].astype(BF16)], axis=1), k_wide, NT
            )
            row_max = jnp.max(scores, axis=1, keepdims=True)
            raised = jnp.exp(scores - row_max).astype(BF16)
            summed = dot(raised, v_wide)
            total = summed[:, LANES:]
            outs.append(summed[:, :LANES] / total)
            mine = ((lane & 15) == 2 * pair + side) & (lane < 48)
            stats = jnp.where(mine, row_max + jnp.log(total), stats)
        out_ref[part] = jnp.where(lane < 64, outs[0], outs[1]).astype(BF16)
        lse_ref[part] = stats

    @pl.when(pair == pairs - 1)
    def _():
        stats = lane_parts(lse_ref[...], lane_q)
        qaug_ref[...] = jnp.where(lane_q < 48, stats, q_mark).astype(BF16)


def attend_forward(triple, segment_col, chunk, rows, block=256):
    keys, width = triple.shape[0], triple.shape[1] // 3
    pairs = width // LANES
    return pl.pallas_call(
        functools.partial(attend_kernel, block=block),
        grid=(pairs,),
        in_specs=[
            pl.BlockSpec((rows, LANES), lambda p: (chunk, p)),
            pl.BlockSpec((keys, LANES), lambda p: (0, pairs + p)),
            pl.BlockSpec((keys, LANES), lambda p: (0, 2 * pairs + p)),
            pl.BlockSpec((rows, 1), lambda p: (chunk, 0)),
            pl.BlockSpec((keys, 1), lambda p: (0, 0)),
        ],
        out_specs=[
            pl.BlockSpec((rows, LANES), lambda p: (0, p)),
            pl.BlockSpec((rows, LANES), lambda p: (0, 0)),
        ],
        out_shape=[
            jax.ShapeDtypeStruct((rows, width), BF16),
            jax.ShapeDtypeStruct((rows, LANES), BF16),
        ],
        scratch_shapes=[pltpu.VMEM((rows, LANES), F32)],
        compiler_params=params(),
        cost_estimate=lasting(14),
        name="attend_forward",
    )(triple, triple, triple, segment_col, segment_col)


def attend_back_kernel(q_ref, k_ref, v_ref, g_ref, seg_ref, qaug_ref, gaug_ref, out_ref, *, block, first_head):
    pair = pl.program_id(0)
    rows = q_ref.shape[0]
    lane = lax.broadcasted_iota(jnp.int32, (block, LANES), 1)
    zero = jnp.asarray(0, BF16)
    query = q_ref[...] * jnp.asarray(0.125, BF16)
    grad = g_ref[...]
    q_wide = jnp.concatenate([query, qaug_ref[...]], axis=1)
    g_wide = jnp.concatenate([grad, gaug_ref[...]], axis=1)
    zone = (lane >= 48) & (lane < 56)
    grad_q = [jnp.zeros((64, rows), F32), jnp.zeros((64, rows), F32)]
    for start in range(0, rows, block):
        part = slice(start, start + block)
        key, value = k_ref[part], v_ref[part]
        key_turned = key.T
        doc = zone & ((lane - 48) == seg_ref[part])
        grads_k, grads_v = [], []
        for side in range(2):
            own = (lane >= 64) if side else (lane < 64)
            stat = ((lane & 15) == first_head + 2 * pair + side) & (lane < 48)
            k_mark = jnp.where(stat, -1.0, jnp.where(doc, 1.0, 0.0)).astype(BF16)
            v_mark = jnp.where(stat, -1.0, 0.0).astype(BF16)
            k_wide = jnp.concatenate([jnp.where(own, key, zero), k_mark], axis=1)
            v_wide = jnp.concatenate([jnp.where(own, value, zero), v_mark], axis=1)
            probs = jnp.exp(dot(k_wide, q_wide, NT))
            grad_scores = (probs * dot(v_wide, g_wide, NT)).astype(BF16)
            grads_v.append(dot(probs.astype(BF16), grad))
            grads_k.append(dot(grad_scores, query))
            grad_q[side] = grad_q[side] + dot(
                key_turned[64 * side : 64 * side + 64], grad_scores
            )
        out_ref[1, part] = jnp.where(lane < 64, grads_k[0], grads_k[1]).astype(BF16)
        out_ref[2, part] = jnp.where(lane < 64, grads_v[0], grads_v[1]).astype(BF16)
    out_ref[0] = (jnp.concatenate(grad_q, axis=0) * 0.125).T.astype(BF16)


def attend_backward(triple, grad, segment_col, qaug, gaug, first_head, heads, block=512):
    rows, width = triple.shape[0], triple.shape[1] // 3
    pairs, first = width // LANES, first_head // 2
    pair_of = lambda offset: pl.BlockSpec((rows, LANES), lambda p: (0, offset + p))
    return pl.pallas_call(
        functools.partial(attend_back_kernel, block=block, first_head=first_head),
        grid=(heads // 2,),
        in_specs=[
            pair_of(first),
            pair_of(pairs + first),
            pair_of(2 * pairs + first),
            pair_of(first),
            pl.BlockSpec((rows, 1), lambda p: (0, 0)),
            pl.BlockSpec((rows, LANES), lambda p: (0, 0)),
            pl.BlockSpec((rows, LANES), lambda p: (0, 0)),
        ],
        out_specs=pl.BlockSpec((3, rows, LANES), lambda p: (0, 0, p)),
        out_shape=jax.ShapeDtypeStruct((3, rows, heads * 64), BF16),
        compiler_params=params(),
        cost_estimate=lasting(13),
        name="attend_backward",
    )(triple, triple, triple, grad, segment_col, qaug, gaug)


def qkv_kernel(tok_ref, gain_ref, *refs):
    weights, (normed_ref, triple_ref) = refs[:-2], refs[-2:]
    rows = tok_ref[...].astype(F32)
    scale = lax.rsqrt(jnp.mean(rows * rows, axis=1, keepdims=True) + EPSILON)
    normed = (rows * scale * gain_ref[...]).astype(BF16)
    normed_ref[...] = normed
    start = 0
    for weight in weights:
        stop = min(start + weight.shape[1], triple_ref.shape[1])
        triple_ref[:, start:stop] = dot(normed, weight[:, : stop - start]).astype(BF16)
        start = stop


def qkv(tokens, gain_row, weights, block=256):
    rows, width = tokens.shape
    return pl.pallas_call(
        qkv_kernel,
        grid=(rows // block,),
        in_specs=[pl.BlockSpec((block, width), lambda i: (i, 0)), whole_spec((1, width))]
        + [whole_spec(weight.shape) for weight in weights],
        out_specs=[
            pl.BlockSpec((block, width), lambda i: (i, 0)),
            pl.BlockSpec((block, 3 * width), lambda i: (i, 0)),
        ],
        out_shape=[
            jax.ShapeDtypeStruct((rows, width), BF16),
            jax.ShapeDtypeStruct((rows, 3 * width), BF16),
        ],
        compiler_params=params(),
        cost_estimate=lasting(8),
        name="qkv",
    )(tokens, gain_row, *weights)


def project_kernel(tok_ref, *refs):
    w_ref, gain_ref, hidden_ref, second_ref = refs[-4:]
    attended = jnp.concatenate([ref[...] for ref in refs[:-4]], axis=1)
    hidden = tok_ref[...].astype(F32) + dot(attended, w_ref[...])
    scale = lax.rsqrt(jnp.mean(hidden * hidden, axis=1, keepdims=True) + EPSILON)
    hidden_ref[...] = hidden
    second_ref[...] = (hidden * scale * gain_ref[...]).astype(BF16)


def project(tokens, attended, weights, gain_row, chunk, block=256):
    attended = [attended]
    rows, part = attended[0].shape
    width = tokens.shape[1]
    steps = rows // block
    here = lambda i: (i, 0)
    return pl.pallas_call(
        project_kernel,
        grid=(steps,),
        in_specs=[pl.BlockSpec((block, width), lambda i: (chunk * steps + i, 0))]
        + [pl.BlockSpec((block, part), here)] * len(attended)
        + [whole_spec((width, width)), whole_spec((1, width))],
        out_specs=[pl.BlockSpec((block, width), here), pl.BlockSpec((block, width), here)],
        out_shape=[
            jax.ShapeDtypeStruct((rows, width), F32),
            jax.ShapeDtypeStruct((rows, width), BF16),
        ],
        compiler_params=params(),
        cost_estimate=lasting(4),
        name="project",
    )(tokens, *attended, weights, gain_row)


def routed_gate(second, router, route_col, experts):
    logits = dot(second, router)
    lane = lax.broadcasted_iota(jnp.int32, logits.shape, 1)
    logits = jnp.where(lane < experts, logits, MASKED)
    raised = jnp.exp(logits - jnp.max(logits, axis=1, keepdims=True))
    probs = raised / jnp.sum(raised, axis=1, keepdims=True)
    chosen = lane == route_col
    gate = jnp.sum(jnp.where(chosen, probs, 0.0), axis=1, keepdims=True)
    return probs, chosen, gate


def on_rows(full, run, capacity):
    pl.when(full == 1)(functools.partial(run, capacity))
    pl.when(full == 0)(functools.partial(run, capacity // 2))


def expert_kernel(
    full_ref,
    rows_a,
    rows_b,
    cot_ref,
    route_ref,
    router_ref,
    place_ref,
    place_col_ref,
    w_in_ref,
    w_out_ref,
    act_ref,
    grad_pre_ref,
    x_ref,
    g_ref,
    ret_ref,
    back_ref,
    gate_ref,
    produced,
    grad_rows,
    *,
    experts,
):
    ff, expert = pl.program_id(0), pl.program_id(1)
    slots = x_ref.shape[0]
    capacity = slots // full_ref.shape[1]
    half = capacity // 2

    @pl.when((ff == 0) & (expert == 0))
    def _():
        produced[...] = jnp.zeros_like(produced)
        grad_rows[...] = jnp.zeros_like(grad_rows)
        second = jnp.concatenate([rows_a[...], rows_b[...]], axis=0)
        _, _, gate = routed_gate(second, router_ref[...], route_ref[...], experts)
        gated = (gate * cot_ref[...].astype(F32)).astype(BF16)

        def pack(start):
            part = slice(start, start + half)
            slot = start + lax.broadcasted_iota(jnp.int32, (half, second.shape[0]), 0)
            pick = jnp.where(slot == place_ref[...], 1.0, 0.0).astype(BF16)
            x_ref[part, :] = dot(pick, second).astype(BF16)
            g_ref[part, :] = dot(pick, gated).astype(BF16)

        for owner in range(slots // capacity):
            pack(owner * capacity)
            pl.when(full_ref[0, owner] == 1)(
                functools.partial(pack, owner * capacity + half)
            )

    def run(rows):
        part = pl.ds(pl.multiple_of(expert * capacity, capacity), rows)
        pre = dot(x_ref[part, :], w_in_ref[0])
        grad_act = dot(g_ref[part, :], w_out_ref[0], NT)
        square = pre * pre
        bend = jnp.tanh(pre * (GELU_C + GELU_C * GELU_A * square))
        upper = 0.5 + 0.5 * bend
        act = (pre * upper).astype(BF16)
        inner = pre * (GELU_C + 3.0 * GELU_C * GELU_A * square)
        slope = upper + inner * (0.5 - 0.5 * bend * bend)
        grad_pre = (grad_act * slope).astype(BF16)
        act_ref[part, :] = act
        grad_pre_ref[part, :] = grad_pre
        produced[part, :] += dot(act, w_out_ref[0])
        grad_rows[part, :] += dot(grad_pre, w_in_ref[0], NT)

    on_rows(full_ref[0, expert], run, capacity)

    @pl.when((ff == pl.num_programs(0) - 1) & (expert == pl.num_programs(1) - 1))
    def _():
        count = ret_ref.shape[0]
        slot = lax.broadcasted_iota(jnp.int32, (count, slots), 1)
        pick = jnp.where(slot == place_col_ref[...], 1.0, 0.0).astype(BF16)
        returned = dot(pick, produced[...].astype(BF16))
        ret_ref[...] = returned.astype(BF16)
        back_ref[...] = dot(pick, grad_rows[...].astype(BF16)).astype(BF16)
        inner = jnp.sum(cot_ref[...].astype(F32) * returned, axis=1, keepdims=True)
        gate_ref[...] = jnp.broadcast_to(inner, gate_ref.shape)


def expert_rows(full, rows, cot, route_col, router, place, w_in, w_out, capacity, experts, ff_block):
    count, width = cot.shape
    local, _, ff = w_in.shape
    slots = local * capacity
    column = lambda f, e, _: (0, f)
    return pl.pallas_call(
        functools.partial(expert_kernel, experts=experts),
        grid_spec=pltpu.PrefetchScalarGridSpec(
            num_scalar_prefetch=1,
            grid=(ff // ff_block, local),
            in_specs=[
                whole_spec(rows[0].shape),
                whole_spec(rows[1].shape),
                whole_spec((count, width)),
                whole_spec((count, 1)),
                whole_spec(router.shape),
                whole_spec((1, count)),
                whole_spec((count, 1)),
                pl.BlockSpec((1, width, ff_block), lambda f, e, _: (e, 0, f)),
                pl.BlockSpec((1, ff_block, width), lambda f, e, _: (e, f, 0)),
            ],
            out_specs=[
                pl.BlockSpec((slots, ff_block), column),
                pl.BlockSpec((slots, ff_block), column),
                whole_spec((slots, width)),
                whole_spec((slots, width)),
                whole_spec((count, width)),
                whole_spec((count, width)),
                whole_spec((count, LANES)),
            ],
            scratch_shapes=[
                pltpu.VMEM((slots, width), F32),
                pltpu.VMEM((slots, width), F32),
            ],
        ),
        out_shape=[
            jax.ShapeDtypeStruct((slots, ff), BF16),
            jax.ShapeDtypeStruct((slots, ff), BF16),
            jax.ShapeDtypeStruct((slots, width), BF16),
            jax.ShapeDtypeStruct((slots, width), BF16),
            jax.ShapeDtypeStruct((count, width), BF16),
            jax.ShapeDtypeStruct((count, width), BF16),
            jax.ShapeDtypeStruct((count, LANES), F32),
        ],
        compiler_params=params(),
        cost_estimate=lasting(28),
        name="expert_rows",
    )(full, *rows, cot, route_col, router, place[None, :], place[:, None], w_in, w_out)


def weight_grad_kernel(full_ref, expert_ref, left_a, left_b, right_a, right_b, out_ref):
    expert = expert_ref[0]
    capacity = left_a.shape[0]

    def run(rows_a, rows_b):
        out_ref[0] = (
            dot(left_a[:rows_a, :], right_a[:rows_a, :], TN)
            + dot(left_b[:rows_b, :], right_b[:rows_b, :], TN)
        ).astype(BF16)

    for full_a in range(2):
        for full_b in range(2):
            pl.when((full_ref[0, expert] == full_a) & (full_ref[1, expert] == full_b))(
                functools.partial(
                    run, capacity // (2 - full_a), capacity // (2 - full_b)
                )
            )


def weight_grad(full, expert, left, right, capacity, ff_block):
    slots, width = left[0].shape
    ff = max(width, right[0].shape[1])
    spec = lambda value: (
        pl.BlockSpec((capacity, ff_block), lambda f, _, e: (e[0], f))
        if value.shape[1] == ff
        else pl.BlockSpec(
            (capacity, value.shape[1]), lambda f, _, e: (e[0], 0), pipeline_mode=pl.Buffered(1)
        )
    )
    block = lambda value: ff_block if value.shape[1] == ff else value.shape[1]
    shape = (block(left[0]), block(right[0]))
    return pl.pallas_call(
        weight_grad_kernel,
        grid_spec=pltpu.PrefetchScalarGridSpec(
            num_scalar_prefetch=2,
            grid=(ff // ff_block,),
            in_specs=[spec(value) for value in (*left, *right)],
            out_specs=pl.BlockSpec((1,) + shape, lambda f, *_: (f, 0, 0)),
        ),
        out_shape=jax.ShapeDtypeStruct((ff // ff_block,) + shape, BF16),
        compiler_params=params(),
        cost_estimate=lasting(9),
        name="weight_grad",
    )(full, expert, *left, *right)


def hidden_back_kernel(
    hidden_a,
    hidden_b,
    second_a,
    second_b,
    cot_ref,
    own_ref,
    sent_ref,
    gate_ref,
    route_ref,
    att_ref,
    router_ref,
    w_ref,
    gain_ref,
    grad_hidden_ref,
    branch_ref,
    grad_att_ref,
    aug_ref,
    gate_out_ref,
    router_grad_ref,
    gain_grad_ref,
    *,
    experts,
):
    @pl.when(pl.program_id(0) == 0)
    def _():
        router_grad_ref[...] = jnp.zeros_like(router_grad_ref)
        gain_grad_ref[...] = jnp.zeros_like(gain_grad_ref)

    early = pl.program_id(0) < pl.num_programs(0) // 2
    hidden = jnp.where(early, hidden_a[...], hidden_b[...])
    second = jnp.where(early, second_a[...], second_b[...])
    cot = cot_ref[...].astype(F32)
    scale = lax.rsqrt(jnp.mean(hidden * hidden, axis=1, keepdims=True) + EPSILON)
    probs, chosen, gate = routed_gate(second, router_ref[...], route_ref[...], experts)
    inner = gate_ref[...]
    gate_out_ref[...] = jnp.broadcast_to(gate, gate_out_ref.shape)
    grad_logits = (probs * (jnp.where(chosen, inner, 0.0) - gate * inner)).astype(BF16)
    router_grad_ref[...] += dot(grad_logits.astype(F32).T.astype(BF16), second)
    grad_second = own_ref[...].astype(F32) + sent_ref[...].astype(F32)
    grad_second = grad_second + dot(grad_logits, router_ref[...], NT)
    scaled_hidden = hidden * scale
    gain_grad_ref[...] += jnp.sum(grad_second * scaled_hidden, axis=0, keepdims=True)
    scaled = grad_second * gain_ref[...]
    mean = jnp.mean(scaled * scaled_hidden, axis=1, keepdims=True)
    grad_hidden = cot + scale * (scaled - scaled_hidden * mean)
    branch = grad_hidden.astype(BF16)
    grad_hidden_ref[...] = grad_hidden
    branch_ref[...] = branch
    grad_att = dot(branch, w_ref[...], NT).astype(BF16)
    grad_att_ref[...] = grad_att
    product = grad_att.astype(F32) * att_ref[...].astype(F32)
    rows, width = product.shape
    feature = lax.broadcasted_iota(jnp.int32, (width, LANES), 0)
    lane = lax.broadcasted_iota(jnp.int32, (width, LANES), 1)
    head = (lane & 15) == feature // 64
    collect = jnp.where(head & (lane < 48), 1.0, 0.0).astype(BF16)
    high = product.astype(BF16)
    rest = product - high.astype(F32)
    middle = rest.astype(BF16)
    low = (rest - middle.astype(F32)).astype(BF16)
    inner = dot(high, collect) + dot(middle, collect) + dot(low, collect)
    row_lane = lax.broadcasted_iota(jnp.int32, (rows, LANES), 1)
    aug_ref[...] = jnp.where(row_lane < 48, lane_parts(inner, row_lane), 0.0).astype(BF16)


def hidden_back(hidden, second, cot, own, sent, inner, route, att, router, weights, gain, experts, block=256):
    rows, width = cot.shape
    steps = rows // block
    half = steps // 2
    here = lambda i: (i, 0)
    wide = lambda index: pl.BlockSpec((block, width), index)
    low = wide(lambda i: (jnp.minimum(i, half - 1), 0))
    high = wide(lambda i: (jnp.maximum(i - half, 0), 0))
    return pl.pallas_call(
        functools.partial(hidden_back_kernel, experts=experts),
        grid=(steps,),
        in_specs=[
            low,
            high,
            low,
            high,
            wide(here),
            wide(here),
            wide(here),
            pl.BlockSpec((block, 1), here),
            pl.BlockSpec((block, 1), here),
            wide(here),
            whole_spec(router.shape),
            whole_spec(weights.shape),
            whole_spec((1, width)),
        ],
        out_specs=[
            wide(here),
            wide(here),
            wide(here),
            pl.BlockSpec((block, LANES), here),
            pl.BlockSpec((block, LANES), here),
            whole_spec((LANES, width)),
            whole_spec((1, width)),
        ],
        out_shape=[
            jax.ShapeDtypeStruct((rows, width), F32),
            jax.ShapeDtypeStruct((rows, width), BF16),
            jax.ShapeDtypeStruct((rows, width), BF16),
            jax.ShapeDtypeStruct((rows, LANES), BF16),
            jax.ShapeDtypeStruct((rows, LANES), F32),
            jax.ShapeDtypeStruct((LANES, width), F32),
            jax.ShapeDtypeStruct((1, width), F32),
        ],
        compiler_params=params(),
        cost_estimate=lasting(12),
        name="hidden_back",
    )(*hidden, *second, cot, own, sent, inner, route, att, router, weights, gain)


def token_back_kernel(tok_ref, grad_ref, gain_ref, *refs):
    weights, triples = refs[:GATHERS], refs[GATHERS:-2]
    out_ref, gain_grad_ref = refs[-2:]

    @pl.when(pl.program_id(0) == 0)
    def _():
        gain_grad_ref[...] = jnp.zeros_like(gain_grad_ref)

    rows = tok_ref[...].astype(F32)
    scale = lax.rsqrt(jnp.mean(rows * rows, axis=1, keepdims=True) + EPSILON)
    grads = jnp.concatenate([t[p] for p in range(3) for t in triples], axis=1)
    grad_normed, start = jnp.zeros(rows.shape, F32), 0
    for weight in weights:
        stop = min(start + weight.shape[1], grads.shape[1])
        grad_normed += dot(grads[:, start:stop], weight[:, : stop - start], NT)
        start = stop
    scaled_rows = rows * scale
    gain_grad_ref[...] += jnp.sum(grad_normed * scaled_rows, axis=0, keepdims=True)
    scaled = grad_normed * gain_ref[...]
    mean = jnp.mean(scaled * scaled_rows, axis=1, keepdims=True)
    out_ref[...] = (grad_ref[...] + scale * (scaled - scaled_rows * mean)).astype(BF16)


def token_back(tokens, grad_hidden, grad_triples, weights, gain_row, block=256):
    rows, width = tokens.shape
    here = lambda i: (i, 0)
    return pl.pallas_call(
        token_back_kernel,
        grid=(rows // block,),
        in_specs=[
            pl.BlockSpec((block, width), here),
            pl.BlockSpec((block, width), here),
            whole_spec((1, width)),
        ]
        + [whole_spec(w.shape) for w in weights]
        + [pl.BlockSpec((3, block, t.shape[2]), lambda i: (0, i, 0)) for t in grad_triples],
        out_specs=[pl.BlockSpec((block, width), here), whole_spec((1, width))],
        out_shape=[
            jax.ShapeDtypeStruct((rows, width), BF16),
            jax.ShapeDtypeStruct((1, width), F32),
        ],
        compiler_params=params(),
        cost_estimate=lasting(9),
        name="token_back",
    )(tokens, grad_hidden, gain_row, *weights, *grad_triples)


def swap(value, axis, step=1):
    size = lax.axis_size(axis)
    return lax.ppermute(value, axis, [(i, i ^ step) for i in range(size)])


def bit_of(axis, step):
    return lax.axis_index(axis) // step % 2


def bits(size, first=1):
    return [1 << n for n in range(first.bit_length() - 1, size.bit_length() - 1)]


def rounded(parts):
    return sum(part.astype(F32) for part in parts).astype(BF16)


def exchange(parts, axis, step, pick):
    bit = bit_of(axis, step)
    give = rounded([pick(part, 1 - bit) for part in parts])
    return [pick(part, bit) for part in parts] + [swap(give, axis, step)]


def halve(parts, axis, step):
    def pick(part, bit):
        parted = part.reshape((part.shape[0], 2, part.shape[1] // 2) + part.shape[2:])
        return lax.dynamic_index_in_dim(parted, bit, 1, keepdims=False)

    return exchange(parts, axis, step, pick)


def to_owner(parts, steps):
    def pick(part, bit):
        parted = part.reshape((part.shape[0] // 2, 2) + part.shape[1:])
        return lax.dynamic_index_in_dim(parted, bit, 1, keepdims=False)

    for step in steps:
        parts = exchange(parts, "shard", step, pick)
    return parts


def to_owner_early(parts):
    return to_owner(parts, bits(lax.axis_size("shard"))[:-1])


def to_owner_last(parts):
    return to_owner(parts, bits(lax.axis_size("shard"))[-1:])


def both(parts, axis, step):
    mine = rounded(parts)
    return [mine, swap(mine, axis, step)]


def unhalve(value, axis, step, dim):
    other = swap(value, axis, step)
    first = bit_of(axis, step) == 0
    low = jnp.where(first, value, other)
    high = jnp.where(first, other, value)
    return jnp.concatenate([low, high], axis=dim)


def neighbours(parts):
    return halve(parts, "dp", 1) if lax.axis_size("dp") > 1 else parts


def spread(parts):
    for step in bits(lax.axis_size("dp"), 2):
        parts = halve(parts, "dp", step)
    return parts


def unspread(value):
    for step in reversed(bits(lax.axis_size("dp"), 2)):
        value = unhalve(value, "dp", step, 0)
    return value


def summed(parts):
    for step in bits(lax.axis_size("dp"), 2):
        parts = both(parts, "dp", step)
    return parts


def finish_expert(early, late, local):
    early, late = rounded(early)[0], rounded(late)[0]
    whole = jnp.concatenate([unspread(early), rounded(summed([late]))], axis=0)
    if lax.axis_size("dp") > 1:
        whole = unhalve(whole, "dp", 1, 0)
    return whole.reshape((local, -1) + whole.shape[1:]).astype(F32)


def tie(value, *sums):
    value, *last = lax.optimization_barrier((value,) + tuple(parts[-1] for parts in sums))
    return (value, *(parts[:-1] + [part] for parts, part in zip(sums, last)))


def dense_near(partial_sum):
    shards = lax.axis_size("shard")
    width, columns = partial_sum.shape
    return neighbours([partial_sum.reshape(shards, width // shards, columns)])


def dense_across(parts):
    return halve(parts, "expert", 1) if lax.axis_size("expert") > 1 else parts


def dense_finish(parts):
    parts = [rounded(to_owner_last(to_owner_early(parts)))[0]]
    for axis in ("expert", "dp"):
        for step in bits(lax.axis_size(axis), 2):
            parts = both(parts, axis, step)
    value = rounded(parts)
    for axis in ("expert", "dp"):
        if lax.axis_size(axis) > 1:
            value = unhalve(value, axis, 1, 0)
    return value.astype(F32)


def gather_rows(value):
    shards, parts = lax.axis_size("shard"), lax.axis_size("dp")
    rows, columns = value.shape
    parted = value.reshape(parts, rows // parts, columns)
    mine = lax.dynamic_index_in_dim(parted, lax.axis_index("dp"), 0, keepdims=False)
    me = lax.axis_index("shard")
    whole = lax.dynamic_update_index_in_dim(
        jnp.zeros((shards,) + mine.shape, value.dtype), mine, me, 0
    )
    for away in range(1, shards):
        piece = lax.ppermute(mine, "shard", [(i, (i + away) % shards) for i in range(shards)])
        whole = lax.dynamic_update_index_in_dim(whole, piece, (me - away) % shards, 0)
    whole = whole[:, None]
    for step in reversed(bits(parts)):
        other = swap(whole, "dp", step)
        first = bit_of("dp", step) == 0
        low, high = jnp.where(first, whole, other), jnp.where(first, other, whole)
        whole = jnp.stack([low, high], axis=2)
        whole = whole.reshape((shards, -1) + mine.shape)
    return whole.reshape(shards * rows, columns)


def places_of(route_ids, first, local, capacity):
    owned = route_ids - first
    choose = owned[:, None] == jnp.arange(local, dtype=jnp.int32)[None, :]
    rank = jnp.cumsum(choose.astype(jnp.int32), axis=0) - 1
    slot = jnp.sum(jnp.where(choose, rank, 0), axis=1) + owned * capacity
    full = (rank[-1] >= capacity // 2).astype(jnp.int32)
    return jnp.where(jnp.any(choose, axis=1), slot, -1), full


def experts_of_pairs(second, cotangent, routes, router, expert_in, expert_out, early):
    rows, width = cotangent.shape
    local, _, ff = expert_in.shape
    experts = router.shape[1]
    router = jnp.pad(router, ((0, 0), (0, LANES - experts)))
    capacity = 2 * rows // experts
    ff_block = ff // lax.axis_size("shard")
    other_cot, other_routes = early
    other_second = [swap(part, "expert") for part in second]
    first_own = lax.axis_index("expert") * local
    results, flags = [], []
    for rows_of, cot, route_ids in (
        (second, cotangent, routes[:, 0]),
        (other_second, other_cot, other_routes),
    ):
        place, full = places_of(route_ids, first_own, local, capacity)
        results.append(
            expert_rows(
                full[None],
                rows_of,
                cot,
                route_ids[:, None],
                router,
                place,
                expert_in,
                expert_out,
                capacity,
                experts,
                ff_block,
            )
        )
        flags.append(full)
    own, other = results
    full = jnp.stack(flags)
    back = [swap(part, "expert") for part in jnp.split(other[5], 2, axis=0)]
    inner = own[6][:, 0] + swap(other[6][:, 0], "expert")
    keep = bit_of("dp", 1)
    one = lambda expert: expert[None].astype(jnp.int32)
    grad = lambda expert, left, right: weight_grad(
        full, one(expert), left, right, capacity, ff_block
    )
    acts, grads = (own[0], other[0]), (own[3], other[3])
    xs, grad_pres = (own[2], other[2]), (own[1], other[1])
    out_give = grad(1 - keep, acts, grads)
    out_sent = swap(out_give, "dp")
    full, _ = lax.optimization_barrier((full, out_give))
    out_keep = grad(keep, acts, grads)
    full, _, back[0] = lax.optimization_barrier((full, out_keep, back[0]))
    in_give = grad(1 - keep, xs, grad_pres)
    in_sent = swap(in_give, "dp")
    full, _, out_sent = lax.optimization_barrier((full, in_give, out_sent))
    in_keep = grad(keep, xs, grad_pres)
    inner, _ = lax.optimization_barrier((inner, in_keep))
    returned = (own[4], swap(other[4], "expert"))
    back = jnp.concatenate(back, axis=0)
    return returned, (own[5], back), inner[:, None], [in_keep, in_sent], [out_keep, out_sent]


def experts_of_many(second, cotangent, routes, router, expert_in, expert_out):
    second = jnp.concatenate(second, axis=0)
    tok_rows, width = second.shape
    experts_all = router.shape[1]
    local, _, ff = expert_in.shape
    groups = lax.axis_size("expert")
    shards = lax.axis_size("shard")
    capacity = 2 * tok_rows // experts_all
    route_ids = routes[:, 0]
    choose = route_ids[:, None] == jnp.arange(experts_all, dtype=jnp.int32)[None, :]
    rank = jnp.cumsum(choose.astype(jnp.int32), axis=0) - 1
    slot_index = route_ids * capacity + jnp.sum(jnp.where(choose, rank, 0), axis=1)
    probs = jax.nn.softmax(dot(second, router), axis=-1)
    gate = jnp.sum(jnp.where(choose, probs, 0.0), axis=1)

    def across(value):
        return lax.all_to_all(value, "expert", split_axis=0, concat_axis=0, tiled=True)

    def to_slots(token_rows):
        filled = jnp.zeros((experts_all * capacity, width), token_rows.dtype)
        filled = filled.at[slot_index].set(token_rows)
        return across(filled.reshape(groups, local, capacity, width))

    def from_slots(value):
        return across(value).reshape(experts_all * capacity, width)[slot_index]

    def einsum(form, left, right):
        return jnp.einsum(form, left, right, preferred_element_type=F32)

    def gelu(value):
        return jax.nn.gelu(value, approximate=True)

    grad_out = cotangent.astype(F32)
    arrived = to_slots(second)
    pre_act, pull = jax.vjp(gelu, einsum("aecd,edf->aecf", arrived, expert_in))
    activated = pre_act.astype(BF16)
    produced = einsum("aecf,efd->aecd", activated, expert_out).astype(BF16)
    returned = from_slots(produced)
    inner = jnp.sum(grad_out * returned.astype(F32), axis=1)
    grad_arrived = to_slots((gate[:, None] * grad_out).astype(BF16))
    grad_act = einsum("aecd,efd->aecf", grad_arrived, expert_out)
    grad_pre = pull(grad_act)[0].astype(BF16)
    grad_w_out = einsum("aecf,aecd->efd", activated, grad_arrived).astype(BF16)
    grad_w_in = einsum("aecd,aecf->edf", arrived, grad_pre).astype(BF16)
    back = from_slots(einsum("aecf,edf->aecd", grad_pre, expert_in).astype(BF16))
    grad_w_in = grad_w_in.reshape(local, width, shards, ff // shards).transpose(2, 0, 1, 3)
    grad_w_out = grad_w_out.reshape(local, shards, ff // shards, width).transpose(1, 0, 2, 3)
    near = lambda value: neighbours([value.reshape((shards, -1) + value.shape[3:])])
    nothing = jnp.zeros_like(back)
    return (
        (returned, nothing),
        (back, nothing),
        inner[:, None],
        near(grad_w_in),
        near(grad_w_out),
    )


def body(
    tokens,
    segments,
    routes,
    cotangent,
    attn_in,
    attn_out,
    router,
    gain_one,
    gain_two,
    expert_in,
    expert_out,
):
    rows, width = tokens.shape
    experts = router.shape[1]
    local = expert_in.shape[0]
    chunk_rows = rows // CHUNKS
    lanes_of = lambda value: jnp.pad(value[:, None], ((0, 0), (0, LANES - 1)))
    padded = lambda value: jnp.pad(value, ((0, 0), (0, LANES - experts)))
    segment_col = segments[0][:, None]
    pairs_only = lax.axis_size("expert") == local == 2 and lax.axis_size("dp") > 1
    early = None

    span = 3 * width // GATHERS
    pieces = [attn_in[:, g * span : (g + 1) * span] for g in range(GATHERS)]
    pieces[-1] = jnp.concatenate([pieces[-1], lanes_of(gain_one)], axis=1)
    weights = [gather_rows(piece) for piece in pieces]
    first_gain = weights[-1][:, span].astype(F32)[None, :]
    if pairs_only:
        early = (swap(cotangent, "expert"), swap(routes[:, 0], "expert"))
    out_full = gather_rows(
        jnp.concatenate([attn_out, padded(router), lanes_of(gain_two)], axis=1)
    )
    full_out = out_full[:, :width]
    full_router = out_full[:, width : width + experts]
    lane_router = out_full[:, width : width + LANES]
    second_gain = out_full[:, width + LANES].astype(F32)[None, :]

    normed, triple = qkv(tokens, first_gain, weights)
    attended, qaug, hidden, second = [], [], [], []
    for chunk in range(CHUNKS):
        att, aug = attend_forward(triple, segment_col, chunk, chunk_rows)
        hid, sec = project(tokens, att, full_out, second_gain, chunk)
        attended.append(att)
        qaug.append(aug)
        hidden.append(hid)
        second.append(sec)
    if pairs_only:
        done = experts_of_pairs(
            second, cotangent, routes, full_router, expert_in, expert_out, early
        )
    else:
        done = experts_of_many(second, cotangent, routes, full_router, expert_in, expert_out)
    returned, backs, inner, in_near, out_near = done

    cut = out_near[0].shape[1] // 3 * 2
    first_part = lambda parts: [part[:, :cut] for part in parts]
    last_part = lambda parts: [part[:, cut:] for part in parts]
    attended_all = jnp.concatenate(attended, axis=0)
    inner, out_near = tie(inner, out_near)
    out_early = spread(first_part(out_near))
    out_late = to_owner_early(last_part(out_near))
    grad_hidden, branch, grad_att, gaug, gates, grad_router, grad_gain_two = hidden_back(
        hidden,
        second,
        cotangent,
        *backs,
        inner,
        routes,
        attended_all,
        lane_router,
        full_out,
        second_gain,
        experts,
    )
    qaug_all = jnp.concatenate(qaug, axis=0)
    heads = width // 64 // GROUPS
    back = lambda grad, g: attend_backward(
        triple, grad, segment_col, qaug_all, gaug, g * heads, heads
    )
    weigh = lambda grads: jnp.einsum(
        "td,pte->dpe", normed, grads, preferred_element_type=F32
    ).reshape(width, -1).astype(BF16)

    grad_att, in_near = tie(grad_att, in_near)
    in_late = to_owner_early(last_part(in_near))
    grads_0 = back(grad_att, 0)
    grad_attn_out = jnp.einsum("td,te->de", attended_all, branch, preferred_element_type=F32)
    dense_a = [
        grad_attn_out.astype(BF16),
        padded(grad_router[:experts].T.astype(BF16)),
        lanes_of(grad_gain_two[0].astype(BF16)),
        weigh(grads_0),
    ]
    dense_a = dense_near(jnp.concatenate(dense_a, axis=1))

    grad_att, out_late, (grads_0,) = tie(grad_att, out_late, [grads_0])
    out_late = to_owner_last(out_late)
    grads_1 = back(grad_att, 1)

    grad_att, out_early, dense_a, (grads_1,) = tie(grad_att, out_early, dense_a, [grads_1])
    out_early = to_owner_early(out_early)
    in_early = spread(first_part(in_near))
    dense_a = dense_across(dense_a)
    grads_2 = back(grad_att, 2)

    grad_hidden, out_early, out_late, in_late, dense_a, (grads_2,) = tie(
        grad_hidden, out_early, out_late, in_late, dense_a, [grads_2]
    )
    out_early = to_owner_last(out_early)
    in_late = to_owner_last(in_late)
    grad_tokens, grad_gain_one = token_back(
        tokens, grad_hidden, (grads_0, grads_1, grads_2), weights, first_gain
    )
    dense_b = [weigh(grads_1), weigh(grads_2), lanes_of(grad_gain_one[0].astype(BF16))]
    dense_b = dense_near(jnp.concatenate(dense_b, axis=1))
    dense_a = dense_finish(dense_a)
    dense_b = dense_finish(dense_across(dense_b))
    final_out = finish_expert(out_early, out_late, local)
    in_early = to_owner_last(to_owner_early(in_early))
    final_in = finish_expert(in_early, in_late, local)

    part = width // GROUPS
    start = width + 2 * LANES
    by_group = [dense_a[:, start:], dense_b[:, : 3 * part], dense_b[:, 3 * part : 6 * part]]
    grad_attn_in = jnp.concatenate(
        [value[:, p * part : (p + 1) * part] for p in range(3) for value in by_group], axis=1
    )

    wide = returned[0].astype(F32) + returned[1].astype(F32)
    layer = jnp.concatenate(hidden, axis=0) + gates[:, :1] * wide
    return (
        layer.astype(BF16),
        grad_tokens,
        grad_attn_in,
        dense_a[:, :width],
        dense_a[:, width : width + experts],
        dense_b[:, 6 * part],
        dense_a[:, width + LANES],
        final_in,
        final_out,
    )


def solution(mesh):
    everywhere = P(("dp", "expert", "shard"), None)
    placed = (everywhere,) * 4 + (P("shard", None),) * 3 + (P("shard"),) * 2
    placed = placed + (P("expert", None, None),) * 2
    outs = (everywhere,) * 2 + (P("shard", None),) * 3 + (P("shard"),) * 2
    outs = outs + (P("expert", None, "shard"), P("expert", "shard", None))
    return jax.shard_map(
        body, mesh=mesh, in_specs=placed, out_specs=outs, check_vma=False
    )
```

time: 1090 us -> 559 us (0.51)
  waiting for transfers between devices: 410 us -> 109 us
  matrix products: 294 us -> 11.8 us
  Pallas kernels: 0 us -> 207 us
  blocking collectives: 123 us -> 0 us
  starting transfers between devices: 8.43 us -> 82.2 us
  other arithmetic: 134 us -> 71.1 us
  local copies, waits for them, and re-layouts: 100 us -> 65.6 us
  between operations: 16.5 us -> 2.15 us
    dot_general x27 -> x4, matrix products: 294 us -> 11.8 us  [the longest x3 7.39 us: body(): jnp.einsum('td,pte->dpe', normed, grads, preferred_element_type=F32)]
    reduce_scatter x4 -> x0, waiting for transfers between devices: 225 us -> none  [the longest x1 116 us: body(): lax.psum_scatter(spread_in.astype(jnp.bfloat16), ('dp', 'shard'), scatter...]
    pallas_call x0 -> x16, Pallas kernels: none -> 207 us  [the longest x2 63.8 us: expert_rows(): pl.pallas_call(functools.partial(expert_kernel, experts=experts), grid_sp...]
    ppermute x0 -> x55, waiting for transfers between devices: none -> 109 us  [the longest x46 102 us: swap(): return lax.ppermute(value, axis, [(i, i ^ step) for i in range(size)])]
    all_gather x4 -> x0, waiting for transfers between devices: 93.9 us -> none  [the longest x1 50.6 us: body(): lax.all_gather(attn_in, 'shard', axis=0, tiled=True)]
    ppermute x0 -> x55, starting transfers between devices: none -> 82.2 us  [the longest x46 70.5 us: swap(): return lax.ppermute(value, axis, [(i, i ^ step) for i in range(size)])]
    all_to_all x2 -> x0, blocking collectives: 77.4 us -> none  [the longest x1 39.7 us: body(): lax.all_to_all(row_slots, 'expert', split_axis=0, concat_axis=0, tiled=True)]
    sub x2 -> x3, other arithmetic: 66 us -> 0.76 us  [the longest x2 0.76 us: places_of(): rank = jnp.cumsum(choose.astype(jnp.int32), axis=0) - 1]
  transfers between devices with their start and end apart: 12 -> 55, of which waited for: 9 -> 17; matrix products, arithmetic and copies ran while one was open for 32% -> 25% of each run, Pallas kernels for 0% -> 30%
where the time goes in v1:
time: 559 us; the launch traced here: 549 us
  Pallas kernels  207 us (37%)
  waiting for transfers between devices  109 us (19%)
  starting transfers between devices  82.2 us (15%)
  other arithmetic  71.1 us (13%)
  local copies, waits for them, and re-layouts  65.6 us (12%)
  matrix products  11.8 us (2%)
    ppermute x46, waiting for transfers between devices, swap(): return lax.ppermute(value, axis, [(i, i ^ step) for i in range(size)])  102 us
    ppermute x46, starting transfers between devices, swap(): return lax.ppermute(value, axis, [(i, i ^ step) for i in range(size)])  70.5 us
    pallas_call x2, Pallas kernels, expert_rows(): pl.pallas_call(functools.partial(expert_kernel, experts=experts), grid_sp...  63.8 us
    pallas_call x3, Pallas kernels, attend_backward(): pl.pallas_call(functools.partial(attend_back_kernel, block=block, first_h...  40.9 us
    pallas_call x4, Pallas kernels, weight_grad(): pl.pallas_call(weight_grad_kernel, grid_spec=pltpu.PrefetchScalarGridSpec...  34.9 us
    pallas_call x2, Pallas kernels, attend_forward(): pl.pallas_call(functools.partial(attend_kernel, block=block), grid=(pairs...  29.3 us
    convert_element_type x20, other arithmetic, rounded(): return sum((part.astype(F32) for part in parts)).astype(BF16)  26.3 us
    dynamic_slice x10, local copies, waits for them, and re-layouts, pick(): return lax.dynamic_index_in_dim(parted, bit, 1, keepdims=False)  12.3 us
  transfers between devices with their start and end apart: 55, of which 17 were waited for; matrix products, arithmetic and copies ran while one was open for 25% of the time, Pallas kernels for 30%

profile of v1, /device:TPU:1, one launch (start us, length us, event | category | flops | bytes accessed | tf_op | source)
XLA Modules:
  0.0 548.5 jit_solution(11092728711324529363)
XLA Ops:
  50.9 6.5 %collective-permute-start.9 = (bf16[4,2,48,1152]{3,2,1,0:T(8,128)(2,1)S(1)}, bf16[4,2,48,1152]{3,2,1,0:T(8,128)(2,1)S(1)}, u32[]{:S(2)}, u32[]{:S(2)}) collective-permute-start(bf16[4,2,48,1152]{3,2,1,0:T(8,128)(2,1)S(1)} %maximum_bitcast_fusion.1), channel_id=1, source_target_pairs={{0,8},{8,0},{16,24},{24,16},{1,9},{9,1},{17,25},{25,17},{2,10},{10... | collective-permute-start | bytes 2654216 | tf_op jit(solution)/shard_map/ppermute | solution.py:609
  70.5 8.4 %qkv.1 = (bf16[1024,768]{1,0:T(8,128)(2,1)}, bf16[1024,2304]{1,0:T(8,128)(2,1)}) custom-call(bf16[1024,768]{1,0:T(8,128)(2,1)} %tok_ref.7, f32[1,768]{1,0:T(1,128)} %reshape.1089.gain_ref, bf16[768,1152]{1,0:T(8,128)(2,1)} %bitcast.304, bf16[768,1280]{1,0:T(8,128)(2,1)} %bitcast.302), custom_call_target="tpu_custom_call" | custom-call | flops 1104000000 | tf_op jit(solution)/shard_map/qkv/pallas_call | solution.py:202
  78.9 14.6 %attend_forward.3 = (bf16[512,768]{1,0:T(8,128)(2,1)}, bf16[512,128]{1,0:T(8,128)(2,1)}) custom-call(bf16[1024,2304]{1,0:T(8,128)(2,1)} %get-tuple-element.65.q_ref.k_ref.v_ref, bf16[1024,2304]{1,0:T(8,128)(2,1)} %get-tuple-element.65.q_ref.k_ref.v_ref, bf16[1024,2304]{1,0:T(8,128)(2,1)} %get-tuple-element.65.q_ref.k_ref.v_ref, ...), custom_call_target="tpu_custom_call" | custom-call | flops 1932000000 | tf_op jit(solution)/shard_map/attend_forward/pallas_call | solution.py:102
  98.4 14.7 %attend_forward.2 = (bf16[512,768]{1,0:T(8,128)(2,1)}, bf16[512,128]{1,0:T(8,128)(2,1)}) custom-call(bf16[1024,2304]{1,0:T(8,128)(2,1)} %get-tuple-element.65.q_ref.k_ref.v_ref, bf16[1024,2304]{1,0:T(8,128)(2,1)} %get-tuple-element.65.q_ref.k_ref.v_ref, bf16[1024,2304]{1,0:T(8,128)(2,1)} %get-tuple-element.65.q_ref.k_ref.v_ref, ...), custom_call_target="tpu_custom_call" | custom-call | flops 1932000000 | tf_op jit(solution)/shard_map/attend_forward/pallas_call | solution.py:102
  122.7 33.4 %expert_rows.2 = (bf16[1024,3072]{1,0:T(8,128)(2,1)}, bf16[1024,3072]{1,0:T(8,128)(2,1)}, bf16[1024,768]{1,0:T(8,128)(2,1)}, bf16[1024,768]{1,0:T(8,128)(2,1)}, ...) custom-call(s32[1,2]{1,0:T(1,128)} %copy-done.55, ...), custom_call_target="tpu_custom_call" | custom-call | flops 3864000000 | tf_op jit(solution)/shard_map/expert_rows/pallas_call | solution.py:353
  157.1 30.4 %expert_rows.3 = (bf16[1024,3072]{1,0:T(8,128)(2,1)}, bf16[1024,3072]{1,0:T(8,128)(2,1)}, bf16[1024,768]{1,0:T(8,128)(2,1)}, bf16[1024,768]{1,0:T(8,128)(2,1)}, ...) custom-call(s32[1,2]{1,0:T(1,128)} %compare_convert_fusion.full_ref, ...), custom_call_target="tpu_custom_call" | custom-call | flops 3864000000 | tf_op jit(solution)/shard_map/expert_rows/pallas_call | solution.py:353
  187.5 9.3 %weight_grad.4 = bf16[4,768,768]{2,1,0:T(8,128)(2,1)} custom-call(s32[2,2]{1,0:T(2,128)} %pad_add_fusion.full_ref, s32[1]{0:T(128)} %bitcast.58.expert_ref, bf16[1024,3072]{1,0:T(8,128)(2,1)} %get-tuple-element.73.left_a, bf16[1024,3072]{1,0:T(8,128)(2,1)} %get-tuple-element.74.left_b, bf16[1024,768]{1,0:T(8,128)(2,1)} %get-tuple-element.75.right_a, ...), custom_call_target="tpu_custom_call" | custom-call | flops 1242000000 | tf_op jit(solution)/shard_map/weight_grad/pallas_call | solution.py:429
  202.9 8.1 %weight_grad.5 = bf16[4,768,768]{2,1,0:T(8,128)(2,1)} custom-call(s32[2,2]{1,0:T(2,128)} %pad_add_fusion.full_ref, s32[1]{0:T(128)} %bitcast.63.expert_ref, bf16[1024,3072]{1,0:T(8,128)(2,1)} %get-tuple-element.73.left_a, bf16[1024,3072]{1,0:T(8,128)(2,1)} %get-tuple-element.74.left_b, bf16[1024,768]{1,0:T(8,128)(2,1)} %get-tuple-element.75.right_a, ...), custom_call_target="tpu_custom_call" | custom-call | flops 1242000000 | tf_op jit(solution)/shard_map/weight_grad/pallas_call | solution.py:429
  211.1 10.0 %collective-permute-done.19 = bf16[512,768]{1,0:T(8,128)(2,1)S(1)} collective-permute-done((bf16[512,768]{1,0:T(8,128)(2,1)}, bf16[512,768]{1,0:T(8,128)(2,1)S(1)}, u32[]{:S(2)}, u32[]{:S(2)}) %collective-permute-start.19) | collective-permute-done | bytes 786464 | tf_op jit(solution)/shard_map/ppermute | solution.py:609
  221.1 9.3 %weight_grad.6 = bf16[4,768,768]{2,1,0:T(8,128)(2,1)} custom-call(s32[2,2]{1,0:T(2,128)} %pad_add_fusion.full_ref, s32[1]{0:T(128)} %bitcast.58.expert_ref, bf16[1024,768]{1,0:T(8,128)(2,1)} %get-tuple-element.83.left_a, bf16[1024,768]{1,0:T(8,128)(2,1)} %get-tuple-element.84.left_b, bf16[1024,3072]{1,0:T(8,128)(2,1)} %get-tuple-element.85.right_a, ...), custom_call_target="tpu_custom_call" | custom-call | flops 1242000000 | tf_op jit(solution)/shard_map/weight_grad/pallas_call | solution.py:429
  244.9 8.1 %collective-permute-done.21 = f32[1024]{0:T(1024)S(1)} collective-permute-done((f32[1024]{0:T(1024)S(1)}, f32[1024]{0:T(1024)S(1)}, u32[]{:S(2)}, u32[]{:S(2)}) %collective-permute-start.21) | collective-permute-done | bytes 4128 | tf_op jit(solution)/shard_map/ppermute | solution.py:609
  254.3 8.1 %weight_grad.7 = bf16[4,768,768]{2,1,0:T(8,128)(2,1)} custom-call(s32[2,2]{1,0:T(2,128)} %pad_add_fusion.full_ref, s32[1]{0:T(128)} %bitcast.63.expert_ref, bf16[1024,768]{1,0:T(8,128)(2,1)} %get-tuple-element.83.left_a, bf16[1024,768]{1,0:T(8,128)(2,1)} %get-tuple-element.84.left_b, bf16[1024,3072]{1,0:T(8,128)(2,1)} %get-tuple-element.85.right_a, ...), custom_call_target="tpu_custom_call" | custom-call | flops 1242000000 | tf_op jit(solution)/shard_map/weight_grad/pallas_call | solution.py:429
  281.6 12.2 %hidden_back.1 = (f32[1024,768]{1,0:T(8,128)}, bf16[1024,768]{1,0:T(8,128)(2,1)}, bf16[1024,768]{1,0:T(8,128)(2,1)}, bf16[1024,128]{1,0:T(8,128)(2,1)}, f32[1024...) custom-call(f32[512,768]{1,0:T(8,128)} %get-tuple-element.67.hidden_a, f32[512,768]{1,0:T(8,128)} %get-tuple-element.69.hidden_b, ...), custom_call_target="tpu_custom_call" | custom-call | flops 1656000000 | tf_op jit(solution)/shard_map/hidden_back/pallas_call | solution.py:518
  299.6 13.8 %attend_backward.3.refs_2_ = bf16[3,1024,256]{2,1,0:T(8,128)(2,1)} custom-call(bf16[1024,2304]{1,0:T(8,128)(2,1)} %get-tuple-element.65.q_ref.k_ref.v_ref, bf16[1024,2304]{1,0:T(8,128)(2,1)} %get-tuple-element.65.q_ref.k_ref.v_ref, bf16[1024,2304]{1,0:T(8,128)(2,1)} %get-tuple-element.65.q_ref.k_ref.v_ref, bf16[1024,768]{1,0:T(8,128)(2,1)} %get-tuple-element.110.g_ref, ...), custom_call_target="tpu_custom_call" | custom-call | flops 1794000000 | tf_op jit(solution)/shard_map/attend_backward/pallas_call | solution.py:167
  345.0 13.7 %attend_backward.4.refs_3_ = bf16[3,1024,256]{2,1,0:T(8,128)(2,1)} custom-call(bf16[1024,2304]{1,0:T(8,128)(2,1)} %get-tuple-element.65.q_ref.k_ref.v_ref, bf16[1024,2304]{1,0:T(8,128)(2,1)} %get-tuple-element.65.q_ref.k_ref.v_ref, bf16[1024,2304]{1,0:T(8,128)(2,1)} %get-tuple-element.65.q_ref.k_ref.v_ref, bf16[1024,768]{1,0:T(8,128)(2,1)} %get-tuple-element.110.g_ref, ...), custom_call_target="tpu_custom_call" | custom-call | flops 1794000000 | tf_op jit(solution)/shard_map/attend_backward/pallas_call | solution.py:167
  372.9 13.4 %attend_backward.5.refs_4_ = bf16[3,1024,256]{2,1,0:T(8,128)(2,1)} custom-call(bf16[1024,2304]{1,0:T(8,128)(2,1)} %get-tuple-element.65.q_ref.k_ref.v_ref, bf16[1024,2304]{1,0:T(8,128)(2,1)} %get-tuple-element.65.q_ref.k_ref.v_ref, bf16[1024,2304]{1,0:T(8,128)(2,1)} %get-tuple-element.65.q_ref.k_ref.v_ref, bf16[1024,768]{1,0:T(8,128)(2,1)} %get-tuple-element.110.g_ref, ...), custom_call_target="tpu_custom_call" | custom-call | flops 1794000000 | tf_op jit(solution)/shard_map/attend_backward/pallas_call | solution.py:167
  396.8 9.7 %token_back.1 = (bf16[1024,768]{1,0:T(8,128)(2,1)}, f32[1,768]{1,0:T(1,128)}) custom-call(bf16[1024,768]{1,0:T(8,128)(2,1)} %tok_ref.7, f32[1024,768]{1,0:T(8,128)} %get-tuple-element.111.grad_ref, f32[1,768]{1,0:T(1,128)} %reshape.1089.gain_ref, bf16[768,1152]{1,0:T(8,128)(2,1)} %bitcast.305, bf16[768,1280]{1,0:T(8,128)(2,1)} %bitcast.303, ...), custom_call_target="tpu_custom_call" | custom-call | flops 1242000000 | tf_op jit(solution)/shard_map/token_back/pallas_call | solution.py:586
  425.7 21.6 %collective-permute-done.51 = bf16[1,256,768]{2,1,0:T(8,128)(2,1)S(1)} collective-permute-done((bf16[1,256,768]{2,1,0:T(8,128)(2,1)S(1)}, bf16[1,256,768]{2,1,0:T(8,128)(2,1)S(1)}, u32[]{:S(2)}, u32[]{:S(2)}) %collective-permute-start.51) | collective-permute-done | bytes 393248 | tf_op jit(solution)/shard_map/ppermute | solution.py:609
  448.7 10.6 %collective-permute-done.48 = bf16[1,256,768]{2,1,0:T(8,128)(2,1)S(1)} collective-permute-done((bf16[1,256,768]{2,1,0:T(8,128)(2,1)S(1)}, bf16[1,256,768]{2,1,0:T(8,128)(2,1)S(1)}, u32[]{:S(2)}, u32[]{:S(2)}) %collective-permute-start.48) | collective-permute-done | bytes 393248 | tf_op jit(solution)/shard_map/ppermute | solution.py:609
  462.2 9.3 %collective-permute-done.33 = bf16[1,48,1792]{2,1,0:T(8,128)(2,1)S(1)} collective-permute-done((bf16[1,48,1792]{2,1,0:T(8,128)(2,1)S(1)}, bf16[1,48,1792]{2,1,0:T(8,128)(2,1)S(1)}, u32[]{:S(2)}, u32[]{:S(2)}) %collective-permute-start.33) | collective-permute-done | bytes 172064 | tf_op jit(solution)/shard_map/ppermute | solution.py:609
  480.6 7.8 %collective-permute-start.54 = (bf16[768,768]{1,0:T(8,128)(2,1)}, bf16[768,768]{1,0:T(8,128)(2,1)}, u32[]{:S(2)}, u32[]{:S(2)}) collective-permute-start(bf16[768,768]{1,0:T(8,128)(2,1)} %pad_maximum_fusion.7), channel_id=1, source_target_pairs={{0,8},{8,0},{16,24},{24,16},{1,9},{9,1},{17,25},{25,17},{2,10},{10... | collective-permute-start | bytes 3538952 | tf_op jit(solution)/shard_map/ppermute | solution.py:609
  494.3 14.2 %collective-permute-done.38 = bf16[4,48,1664]{2,1,0:T(8,128)(2,1)S(1)} collective-permute-done((bf16[4,48,1664]{2,1,0:T(8,128)(2,1)S(1)}, bf16[4,48,1664]{2,1,0:T(8,128)(2,1)S(1)}, u32[]{:S(2)}, u32[]{:S(2)}) %collective-permute-start.38) | collective-permute-done | bytes 639008 | tf_op jit(solution)/shard_map/ppermute | solution.py:609
  509.9 6.9 %collective-permute-done.39 = bf16[2,48,1664]{2,1,0:T(8,128)(2,1)S(1)} collective-permute-done((bf16[2,48,1664]{2,1,0:T(8,128)(2,1)S(1)}, bf16[2,48,1664]{2,1,0:T(8,128)(2,1)S(1)}, u32[]{:S(2)}, u32[]{:S(2)}) %collective-permute-start.39) | collective-permute-done | bytes 319520 | tf_op jit(solution)/shard_map/ppermute | solution.py:609
  522.2 6.0 %collective-permute-done.40 = bf16[1,48,1664]{2,1,0:T(8,128)(2,1)} collective-permute-done((bf16[1,48,1664]{2,1,0:T(8,128)(2,1)}, bf16[1,48,1664]{2,1,0:T(8,128)(2,1)}, u32[]{:S(2)}, u32[]{:S(2)}) %collective-permute-start.40) | collective-permute-done | bytes 159776 | tf_op jit(solution)/shard_map/ppermute | solution.py:609
  (394 shorter events, 246.3 us)
Async XLA Ops:
  3.4 27.5 %collective-permute-start.12 = (bf16[48,1024]{1,0:T(8,128)(2,1)S(1)}, bf16[48,1024]{1,0:T(8,128)(2,1)S(1)}, u32[]{:S(2)}, u32[]{:S(2)}) collective-permute-start(bf16[48,1024]{1,0:T(8,128)(2,1)S(1)} %dynamic-slice_bitcast_fusion.4), channel_id=1, source_target_pairs={{0,3},{1,0},{2,1},{3,2},{4,7},{5,4},{6,5},{7,6},{8,11},{9,8},{10,9... | collective-permute-start | bytes 294920 | tf_op jit(solution)/shard_map/ppermute | solution.py:736
  31.6 124.6 %collective-permute-start.18 = (bf16[1024,768]{1,0:T(8,128)(2,1)}, bf16[1024,768]{1,0:T(8,128)(2,1)}, u32[]{:S(2)}, u32[]{:S(2)}) collective-permute-start(bf16[1024,768]{1,0:T(8,128)(2,1)} %cot_ref.3), channel_id=1, source_target_pairs={{0,4},{4,0},{1,5},{5,1},{2,6},{6,2},{3,7},{7,3},{8,12},{12,8},{9,1... | collective-permute-start | bytes 4718600 | tf_op jit(solution)/shard_map/ppermute | solution.py:609
  97.2 59.0 %collective-permute-start.17 = (bf16[512,768]{1,0:T(8,128)(2,1)}, bf16[512,768]{1,0:T(8,128)(2,1)S(1)}, u32[]{:S(2)}, u32[]{:S(2)}) collective-permute-start(bf16[512,768]{1,0:T(8,128)(2,1)} %get-tuple-element.71.rows_b.second_b), channel_id=1, source_target_pairs={{0,4},{4,0},{1,5},{5,1},{2,6},{6,2},{3,7},{7,3},{8,12},{12,8},{9,1... | collective-permute-start | bytes 2359304 | tf_op jit(solution)/shard_map/ppermute | solution.py:609
  116.8 39.4 %collective-permute-start.16 = (bf16[512,768]{1,0:T(8,128)(2,1)}, bf16[512,768]{1,0:T(8,128)(2,1)}, u32[]{:S(2)}, u32[]{:S(2)}) collective-permute-start(bf16[512,768]{1,0:T(8,128)(2,1)} %get-tuple-element.70.rows_a.second_a), channel_id=1, source_target_pairs={{0,4},{4,0},{1,5},{5,1},{2,6},{6,2},{3,7},{7,3},{8,12},{12,8},{9,1... | collective-permute-start | bytes 2359304 | tf_op jit(solution)/shard_map/ppermute | solution.py:609
  196.8 57.4 %collective-permute-start.22 = (bf16[4,768,768]{2,1,0:T(8,128)(2,1)}, bf16[4,768,768]{2,1,0:T(8,128)(2,1)}, u32[]{:S(2)}, u32[]{:S(2)}) collective-permute-start(bf16[4,768,768]{2,1,0:T(8,128)(2,1)} %weight_grad.4), channel_id=1, source_target_pairs={{0,8},{8,0},{16,24},{24,16},{1,9},{9,1},{17,25},{25,17},{2,10},{10... | collective-permute-start | bytes 14155784 | tf_op jit(solution)/shard_map/ppermute | solution.py:609
  230.4 69.2 %collective-permute-start.24 = (bf16[4,768,768]{2,1,0:T(8,128)(2,1)}, bf16[4,768,768]{2,1,0:T(8,128)(2,1)}, u32[]{:S(2)}, u32[]{:S(2)}) collective-permute-start(bf16[4,768,768]{2,1,0:T(8,128)(2,1)} %weight_grad.6), channel_id=1, source_target_pairs={{0,8},{8,0},{16,24},{24,16},{1,9},{9,1},{17,25},{25,17},{2,10},{10... | collective-permute-start | bytes 14155784 | tf_op jit(solution)/shard_map/ppermute | solution.py:609
  242.7 87.8 %collective-permute-start.23 = (bf16[1024,768]{1,0:T(8,128)(2,1)}, bf16[1024,768]{1,0:T(8,128)(2,1)}, u32[]{:S(2)}, u32[]{:S(2)}) collective-permute-start(bf16[1024,768]{1,0:T(8,128)(2,1)} %get-tuple-element.93), channel_id=1, source_target_pairs={{0,4},{4,0},{1,5},{5,1},{2,6},{6,2},{3,7},{7,3},{8,12},{12,8},{9,1... | collective-permute-start | bytes 4718600 | tf_op jit(solution)/shard_map/ppermute | solution.py:609
  272.6 66.0 %collective-permute-start.25 = (bf16[2,256,768]{2,1,0:T(8,128)(2,1)}, bf16[2,256,768]{2,1,0:T(8,128)(2,1)}, u32[]{:S(2)}, u32[]{:S(2)}) collective-permute-start(bf16[2,256,768]{2,1,0:T(8,128)(2,1)} %fusion.28), channel_id=1, source_target_pairs={{0,1},{1,0},{2,3},{3,2},{4,5},{5,4},{6,7},{7,6},{8,9},{9,8},{10,11... | collective-permute-start | bytes 2359304 | tf_op jit(solution)/shard_map/ppermute | solution.py:609
  277.9 83.7 %collective-permute-start.26 = (bf16[4,256,768]{2,1,0:T(8,128)(2,1)}, bf16[4,256,768]{2,1,0:T(8,128)(2,1)}, u32[]{:S(2)}, u32[]{:S(2)}) collective-permute-start(bf16[4,256,768]{2,1,0:T(8,128)(2,1)} %fusion.10), channel_id=1, source_target_pairs={{0,16},{8,24},{16,0},{24,8},{1,17},{9,25},{17,1},{25,9},{2,18},{10... | collective-permute-start | bytes 4718600 | tf_op jit(solution)/shard_map/ppermute | solution.py:609
  326.7 34.8 %collective-permute-start.27 = (bf16[4,96,1792]{2,1,0:T(8,128)(2,1)}, bf16[4,96,1792]{2,1,0:T(8,128)(2,1)}, u32[]{:S(2)}, u32[]{:S(2)}) collective-permute-start(bf16[4,96,1792]{2,1,0:T(8,128)(2,1)} %get-tuple-element.160), channel_id=1, source_target_pairs={{0,8},{8,0},{16,24},{24,16},{1,9},{9,1},{17,25},{25,17},{2,10},{10... | collective-permute-start | bytes 4128776 | tf_op jit(solution)/shard_map/ppermute | solution.py:609
  340.8 53.0 %collective-permute-start.29 = (bf16[1,256,768]{2,1,0:T(8,128)(2,1)S(1)}, bf16[1,256,768]{2,1,0:T(8,128)(2,1)}, u32[]{:S(2)}, u32[]{:S(2)}) collective-permute-start(bf16[1,256,768]{2,1,0:T(8,128)(2,1)S(1)} %fusion.43), channel_id=1, source_target_pairs={{0,2},{1,3},{2,0},{3,1},{4,6},{5,7},{6,4},{7,5},{8,10},{9,11},{10,... | collective-permute-start | bytes 1179656 | tf_op jit(solution)/shard_map/ppermute | solution.py:609
  342.3 51.6 %collective-permute-start.30 = (bf16[2,256,768]{2,1,0:T(8,128)(2,1)}, bf16[2,256,768]{2,1,0:T(8,128)(2,1)}, u32[]{:S(2)}, u32[]{:S(2)}) collective-permute-start(bf16[2,256,768]{2,1,0:T(8,128)(2,1)} %fusion.30), channel_id=1, source_target_pairs={{0,1},{1,0},{2,3},{3,2},{4,5},{5,4},{6,7},{7,6},{8,9},{9,8},{10,11... | collective-permute-start | bytes 2359304 | tf_op jit(solution)/shard_map/ppermute | solution.py:609
  344.7 45.4 %collective-permute-start.44 = (bf16[4,256,768]{2,1,0:T(8,128)(2,1)}, bf16[4,256,768]{2,1,0:T(8,128)(2,1)}, u32[]{:S(2)}, u32[]{:S(2)}) collective-permute-start(bf16[4,256,768]{2,1,0:T(8,128)(2,1)} %fusion.11), channel_id=1, source_target_pairs={{0,16},{8,24},{16,0},{24,8},{1,17},{9,25},{17,1},{25,9},{2,18},{10... | collective-permute-start | bytes 4718600 | tf_op jit(solution)/shard_map/ppermute | solution.py:609
  363.9 29.9 %collective-permute-start.31 = (bf16[4,48,1792]{2,1,0:T(8,128)(2,1)}, bf16[4,48,1792]{2,1,0:T(8,128)(2,1)}, u32[]{:S(2)}, u32[]{:S(2)}) collective-permute-start(bf16[4,48,1792]{2,1,0:T(8,128)(2,1)} %fusion.47), channel_id=1, source_target_pairs={{0,4},{4,0},{1,5},{5,1},{2,6},{6,2},{3,7},{7,3},{8,12},{12,8},{9,1... | collective-permute-start | bytes 2064392 | tf_op jit(solution)/shard_map/ppermute | solution.py:609
  392.8 25.4 %collective-permute-start.45 = (bf16[2,256,768]{2,1,0:T(8,128)(2,1)}, bf16[2,256,768]{2,1,0:T(8,128)(2,1)}, u32[]{:S(2)}, u32[]{:S(2)}) collective-permute-start(bf16[2,256,768]{2,1,0:T(8,128)(2,1)} %fusion.31), channel_id=1, source_target_pairs={{0,1},{1,0},{2,3},{3,2},{4,5},{5,4},{6,7},{7,6},{8,9},{9,8},{10,11... | collective-permute-start | bytes 2359304 | tf_op jit(solution)/shard_map/ppermute | solution.py:609
  412.2 35.0 %collective-permute-start.51 = (bf16[1,256,768]{2,1,0:T(8,128)(2,1)S(1)}, bf16[1,256,768]{2,1,0:T(8,128)(2,1)S(1)}, u32[]{:S(2)}, u32[]{:S(2)}) collective-permute-start(bf16[1,256,768]{2,1,0:T(8,128)(2,1)S(1)} %fusion.34), channel_id=1, source_target_pairs={{0,2},{1,3},{2,0},{3,1},{4,6},{5,7},{6,4},{7,5},{8,10},{9,11},{10,... | collective-permute-start | bytes 1179656 | tf_op jit(solution)/shard_map/ppermute | solution.py:609
  414.4 44.9 %collective-permute-start.48 = (bf16[1,256,768]{2,1,0:T(8,128)(2,1)S(1)}, bf16[1,256,768]{2,1,0:T(8,128)(2,1)S(1)}, u32[]{:S(2)}, u32[]{:S(2)}) collective-permute-start(bf16[1,256,768]{2,1,0:T(8,128)(2,1)S(1)} %fusion.37), channel_id=1, source_target_pairs={{0,2},{1,3},{2,0},{3,1},{4,6},{5,7},{6,4},{7,5},{8,10},{9,11},{10,... | collective-permute-start | bytes 1179656 | tf_op jit(solution)/shard_map/ppermute | solution.py:609
  416.2 45.6 %collective-permute-start.53 = (bf16[256,768]{1,0:T(8,128)(2,1)S(1)}, bf16[256,768]{1,0:T(8,128)(2,1)S(1)}, u32[]{:S(2)}, u32[]{:S(2)}) collective-permute-start(bf16[256,768]{1,0:T(8,128)(2,1)S(1)} %fusion.57), channel_id=1, source_target_pairs={{0,16},{8,24},{16,0},{24,8},{1,17},{9,25},{17,1},{25,9},{2,18},{10... | collective-permute-start | bytes 1179656 | tf_op jit(solution)/shard_map/ppermute | solution.py:609
  418.2 74.0 %collective-permute-start.37 = (bf16[4,96,1664]{2,1,0:T(8,128)(2,1)S(1)}, bf16[4,96,1664]{2,1,0:T(8,128)(2,1)S(1)}, u32[]{:S(2)}, u32[]{:S(2)}) collective-permute-start(bf16[4,96,1664]{2,1,0:T(8,128)(2,1)S(1)} %get-tuple-element.162), channel_id=1, source_target_pairs={{0,8},{8,0},{16,24},{24,16},{1,9},{9,1},{17,25},{25,17},{2,10},{10... | collective-permute-start | bytes 3833864 | tf_op jit(solution)/shard_map/ppermute | solution.py:609
  424.6 49.2 %collective-permute-start.46 = (bf16[1,256,768]{2,1,0:T(8,128)(2,1)S(1)}, bf16[1,256,768]{2,1,0:T(8,128)(2,1)S(1)}, u32[]{:S(2)}, u32[]{:S(2)}) collective-permute-start(bf16[1,256,768]{2,1,0:T(8,128)(2,1)S(1)} %fusion.40), channel_id=1, source_target_pairs={{0,2},{1,3},{2,0},{3,1},{4,6},{5,7},{6,4},{7,5},{8,10},{9,11},{10,... | collective-permute-start | bytes 1179656 | tf_op jit(solution)/shard_map/ppermute | solution.py:609
  447.2 24.2 %collective-permute-start.33 = (bf16[1,48,1792]{2,1,0:T(8,128)(2,1)S(1)}, bf16[1,48,1792]{2,1,0:T(8,128)(2,1)S(1)}, u32[]{:S(2)}, u32[]{:S(2)}) collective-permute-start(bf16[1,48,1792]{2,1,0:T(8,128)(2,1)S(1)} %fusion.59), channel_id=1, source_target_pairs={{0,2},{1,3},{2,0},{3,1},{4,6},{5,7},{6,4},{7,5},{8,10},{9,11},{10,... | collective-permute-start | bytes 516104 | tf_op jit(solution)/shard_map/ppermute | solution.py:609
  461.8 26.6 %collective-permute-start.49 = (bf16[256,768]{1,0:T(8,128)(2,1)S(1)}, bf16[256,768]{1,0:T(8,128)(2,1)S(1)}, u32[]{:S(2)}, u32[]{:S(2)}) collective-permute-start(bf16[256,768]{1,0:T(8,128)(2,1)S(1)} %fusion.55), channel_id=1, source_target_pairs={{0,16},{8,24},{16,0},{24,8},{1,17},{9,25},{17,1},{25,9},{2,18},{10... | collective-permute-start | bytes 1179656 | tf_op jit(solution)/shard_map/ppermute | solution.py:609
  480.6 50.2 %collective-permute-start.54 = (bf16[768,768]{1,0:T(8,128)(2,1)}, bf16[768,768]{1,0:T(8,128)(2,1)}, u32[]{:S(2)}, u32[]{:S(2)}) collective-permute-start(bf16[768,768]{1,0:T(8,128)(2,1)} %pad_maximum_fusion.7), channel_id=1, source_target_pairs={{0,8},{8,0},{16,24},{24,16},{1,9},{9,1},{17,25},{25,17},{2,10},{10... | collective-permute-start | bytes 3538952 | tf_op jit(solution)/shard_map/ppermute | solution.py:609
  493.9 47.7 %collective-permute-start.50 = (bf16[768,768]{1,0:T(8,128)(2,1)}, bf16[768,768]{1,0:T(8,128)(2,1)}, u32[]{:S(2)}, u32[]{:S(2)}) collective-permute-start(bf16[768,768]{1,0:T(8,128)(2,1)} %pad_maximum_fusion.6), channel_id=1, source_target_pairs={{0,8},{8,0},{16,24},{24,16},{1,9},{9,1},{17,25},{25,17},{2,10},{10... | collective-permute-start | bytes 3538952 | tf_op jit(solution)/shard_map/ppermute | solution.py:609
  (90 other events, 968.5 us)

commit v2 on v1

v2 whole, which is shorter than its diff:
```python
import functools
import math

import jax
import jax.numpy as jnp
from jax import lax
from jax.experimental import pallas as pl
from jax.experimental.pallas import tpu as pltpu
from jax.sharding import PartitionSpec as P

HEADS = 12
LANES = 128
EPSILON = 1e-06
MASKED = -1e30
BF16 = jnp.bfloat16
F32 = jnp.float32
NN = (((1,), (0,)), ((), ()))
NT = (((1,), (1,)), ((), ()))
TN = (((0,), (0,)), ((), ()))
GROUPS = 3
GATHERS = 2
SHARE = 0.05
GELU_C = math.sqrt(2.0 / math.pi)
GELU_A = 0.044715


def dot(left, right, dims=NN):
    return lax.dot_general(left, right, dims, preferred_element_type=F32)


def column_of(row):
    wide = jnp.broadcast_to(row.astype(F32), (LANES, row.shape[1]))
    return wide.T.astype(jnp.int32)


def params(mebibytes=60):
    return pltpu.CompilerParams(vmem_limit_bytes=mebibytes << 20)


def lasting(microseconds):
    return pl.CostEstimate(
        flops=int(microseconds * SHARE * 1.15e9), bytes_accessed=0, transcendentals=0
    )


def whole_spec(shape, buffers=1):
    return pl.BlockSpec(
        shape, lambda *_: (0,) * len(shape), pipeline_mode=pl.Buffered(buffers)
    )


def lane_parts(value, lane):
    high = value.astype(BF16).astype(F32)
    middle = (value - high).astype(BF16).astype(F32)
    low = value - high - middle
    return jnp.where(lane < 16, high, jnp.where(lane < 32, middle, low))


def attend_kernel(q_ref, k_ref, v_ref, seg_ref, out_ref, qaug_ref, lse_ref, *, block):
    pair, pairs = pl.program_id(0), pl.num_programs(0)
    rows, keys = q_ref.shape[0], k_ref.shape[0]
    lane_k = lax.broadcasted_iota(jnp.int32, (keys, LANES), 1)
    lane_q = lax.broadcasted_iota(jnp.int32, (rows, LANES), 1)
    k_mark = jnp.where((lane_k - 48) == seg_ref[...], 1.0, 0.0).astype(BF16)
    zone = (lane_q >= 48) & (lane_q < 56)
    q_mark = jnp.where(zone & ((lane_q - 48) != seg_ref[...]), MASKED, 0.0)

    @pl.when(pair == 0)
    def _():
        lse_ref[...] = jnp.zeros_like(lse_ref)

    k_mark = jnp.where((lane_k >= 48) & (lane_k < 56), k_mark, jnp.asarray(0, BF16))
    k_wide = jnp.concatenate([k_ref[...], k_mark], axis=1)
    v_wide = jnp.concatenate([v_ref[...], jnp.ones((keys, LANES), BF16)], axis=1)
    lane = lane_q[:block]
    for start in range(0, rows, block):
        part = slice(start, start + block)
        query = q_ref[part] * jnp.asarray(0.125, BF16)
        outs = []
        stats = lse_ref[part]
        for side in range(2):
            own = (lane >= 64) if side else (lane < 64)
            picked = jnp.where(own, query, jnp.asarray(0, BF16))
            scores = dot(
                jnp.concatenate([picked, q_mark[part].astype(BF16)], axis=1), k_wide, NT
            )
            row_max = jnp.max(scores, axis=1, keepdims=True)
            raised = jnp.exp(scores - row_max).astype(BF16)
            summed = dot(raised, v_wide)
            total = summed[:, LANES:]
            outs.append(summed[:, :LANES] / total)
            mine = ((lane & 15) == 2 * pair + side) & (lane < 48)
            stats = jnp.where(mine, row_max + jnp.log(total), stats)
        out_ref[part] = jnp.where(lane < 64, outs[0], outs[1]).astype(BF16)
        lse_ref[part] = stats

    @pl.when(pair == pairs - 1)
    def _():
        stats = lane_parts(lse_ref[...], lane_q)
        qaug_ref[...] = jnp.where(lane_q < 48, stats, q_mark).astype(BF16)


def attend_forward(triple, segment_col, block=256):
    rows, width = triple.shape[0], triple.shape[1] // 3
    pairs = width // LANES
    return pl.pallas_call(
        functools.partial(attend_kernel, block=block),
        grid=(pairs,),
        in_specs=[
            pl.BlockSpec((rows, LANES), lambda p: (0, p)),
            pl.BlockSpec((rows, LANES), lambda p: (0, pairs + p)),
            pl.BlockSpec((rows, LANES), lambda p: (0, 2 * pairs + p)),
            whole_spec((rows, 1)),
        ],
        out_specs=[
            pl.BlockSpec((rows, LANES), lambda p: (0, p)),
            pl.BlockSpec((rows, LANES), lambda p: (0, 0)),
        ],
        out_shape=[
            jax.ShapeDtypeStruct((rows, width), BF16),
            jax.ShapeDtypeStruct((rows, LANES), BF16),
        ],
        scratch_shapes=[pltpu.VMEM((rows, LANES), F32)],
        compiler_params=params(),
        cost_estimate=lasting(24),
        name="attend_forward",
    )(triple, triple, triple, segment_col)


def keep_and_give(bit, result, keep_ref, give_ref):
    shards, half = keep_ref.shape[0], keep_ref.shape[1]
    result = result.astype(BF16)
    for shard in range(shards):
        low = result[2 * half * shard : 2 * half * shard + half]
        high = result[2 * half * shard + half : 2 * half * shard + 2 * half]
        keep_ref[shard] = jnp.where(bit == 0, low, high)
        give_ref[shard] = jnp.where(bit == 0, high, low)


def attend_back_kernel(
    bit_ref,
    q_ref,
    k_ref,
    v_ref,
    g_ref,
    seg_ref,
    qaug_ref,
    gaug_ref,
    normed_ref,
    out_ref,
    keep_ref,
    give_ref,
    *,
    block,
    first_head,
):
    pair = pl.program_id(0)
    rows = q_ref.shape[0]
    lane = lax.broadcasted_iota(jnp.int32, (block, LANES), 1)
    zero = jnp.asarray(0, BF16)
    query = q_ref[...] * jnp.asarray(0.125, BF16)
    grad = g_ref[...]
    q_wide = jnp.concatenate([query, qaug_ref[...]], axis=1)
    g_wide = jnp.concatenate([grad, gaug_ref[...]], axis=1)
    zone = (lane >= 48) & (lane < 56)
    grad_q = [jnp.zeros((64, rows), F32), jnp.zeros((64, rows), F32)]
    for start in range(0, rows, block):
        part = slice(start, start + block)
        key, value = k_ref[part], v_ref[part]
        key_turned = key.T
        doc = zone & ((lane - 48) == seg_ref[part])
        grads_k, grads_v = [], []
        for side in range(2):
            own = (lane >= 64) if side else (lane < 64)
            stat = ((lane & 15) == first_head + 2 * pair + side) & (lane < 48)
            k_mark = jnp.where(stat, -1.0, jnp.where(doc, 1.0, 0.0)).astype(BF16)
            v_mark = jnp.where(stat, -1.0, 0.0).astype(BF16)
            k_wide = jnp.concatenate([jnp.where(own, key, zero), k_mark], axis=1)
            v_wide = jnp.concatenate([jnp.where(own, value, zero), v_mark], axis=1)
            probs = jnp.exp(dot(k_wide, q_wide, NT))
            grad_scores = (probs * dot(v_wide, g_wide, NT)).astype(BF16)
            grads_v.append(dot(probs.astype(BF16), grad))
            grads_k.append(dot(grad_scores, query))
            grad_q[side] = grad_q[side] + dot(
                key_turned[64 * side : 64 * side + 64], grad_scores
            )
        out_ref[1, part] = jnp.where(lane < 64, grads_k[0], grads_k[1]).astype(BF16)
        out_ref[2, part] = jnp.where(lane < 64, grads_v[0], grads_v[1]).astype(BF16)
    out_ref[0] = (jnp.concatenate(grad_q, axis=0) * 0.125).T.astype(BF16)
    grads = jnp.concatenate([out_ref[0], out_ref[1], out_ref[2]], axis=1)
    keep_and_give(bit_ref[0], dot(normed_ref[...], grads, TN), keep_ref, give_ref)


def attend_backward(bit, triple, grad, segment_col, qaug, gaug, normed, shards, first_head, heads, block=512):
    rows, width = normed.shape
    pairs, first, half = width // LANES, first_head // 2, width // shards // 2
    pair_of = lambda offset: pl.BlockSpec((rows, LANES), lambda p, _: (0, offset + p))
    weight_half = pl.BlockSpec((shards, half, 3 * LANES), lambda p, _: (0, 0, p))
    return pl.pallas_call(
        functools.partial(attend_back_kernel, block=block, first_head=first_head),
        grid_spec=pltpu.PrefetchScalarGridSpec(
            num_scalar_prefetch=1,
            grid=(heads // 2,),
            in_specs=[
                pair_of(first),
                pair_of(pairs + first),
                pair_of(2 * pairs + first),
                pair_of(first),
                whole_spec((rows, 1)),
                whole_spec((rows, LANES)),
                whole_spec((rows, LANES)),
                whole_spec((rows, width)),
            ],
            out_specs=[
                pl.BlockSpec((3, rows, LANES), lambda p, _: (0, 0, p)),
                weight_half,
                weight_half,
            ],
        ),
        out_shape=[
            jax.ShapeDtypeStruct((3, rows, heads * 64), BF16),
            jax.ShapeDtypeStruct((shards, half, heads // 2 * 3 * LANES), BF16),
            jax.ShapeDtypeStruct((shards, half, heads // 2 * 3 * LANES), BF16),
        ],
        compiler_params=params(),
        cost_estimate=lasting(14),
        name="attend_backward",
    )(bit, triple, triple, triple, grad, segment_col, qaug, gaug, normed)


def qkv_kernel(tok_ref, gain_ref, *refs):
    weights, (normed_ref, triple_ref) = refs[:-2], refs[-2:]
    rows = tok_ref[...].astype(F32)
    scale = lax.rsqrt(jnp.mean(rows * rows, axis=1, keepdims=True) + EPSILON)
    normed = (rows * scale * gain_ref[...]).astype(BF16)
    normed_ref[...] = normed
    span = triple_ref.shape[1] // len(weights)
    for at, weight in enumerate(weights):
        triple_ref[:, at * span : (at + 1) * span] = dot(normed, weight[...]).astype(BF16)


def qkv(tokens, gain_row, weights, span, block=256):
    rows, width = tokens.shape
    return pl.pallas_call(
        qkv_kernel,
        grid=(rows // block,),
        in_specs=[pl.BlockSpec((block, width), lambda i: (i, 0)), whole_spec((1, width))]
        + [whole_spec((width, span)) for weight in weights],
        out_specs=[
            pl.BlockSpec((block, width), lambda i: (i, 0)),
            pl.BlockSpec((block, 3 * width), lambda i: (i, 0)),
        ],
        out_shape=[
            jax.ShapeDtypeStruct((rows, width), BF16),
            jax.ShapeDtypeStruct((rows, 3 * width), BF16),
        ],
        compiler_params=params(),
        cost_estimate=lasting(8),
        name="qkv",
    )(tokens, gain_row, *weights)


def project_kernel(tok_ref, att_ref, w_ref, gain_ref, hidden_ref, second_ref):
    hidden = tok_ref[...].astype(F32) + dot(att_ref[...], w_ref[...])
    scale = lax.rsqrt(jnp.mean(hidden * hidden, axis=1, keepdims=True) + EPSILON)
    hidden_ref[...] = hidden
    second_ref[...] = (hidden * scale * gain_ref[...]).astype(BF16)


def project(tokens, attended, out_full, gain_row, block=256):
    rows, width = tokens.shape
    wide = pl.BlockSpec((block, width), lambda i: (i, 0))
    return pl.pallas_call(
        project_kernel,
        grid=(rows // block,),
        in_specs=[wide, wide, whole_spec((width, width)), whole_spec((1, width))],
        out_specs=[wide, wide],
        out_shape=[
            jax.ShapeDtypeStruct((rows, width), F32),
            jax.ShapeDtypeStruct((rows, width), BF16),
        ],
        compiler_params=params(),
        cost_estimate=lasting(7),
        name="project",
    )(tokens, attended, out_full, gain_row)


def routed_gate(second, router, route_wide, experts):
    logits = dot(second, router)
    lane = lax.broadcasted_iota(jnp.int32, logits.shape, 1)
    logits = jnp.where(lane < experts, logits, MASKED)
    raised = jnp.exp(logits - jnp.max(logits, axis=1, keepdims=True))
    probs = raised / jnp.sum(raised, axis=1, keepdims=True)
    chosen = lane == route_wide
    gate = jnp.sum(jnp.where(chosen, probs, 0.0), axis=1, keepdims=True)
    return probs, chosen, gate


def on_rows(full, run, capacity):
    pl.when(full == 1)(functools.partial(run, capacity))
    pl.when(full == 0)(functools.partial(run, capacity // 2))


def expert_kernel(
    full_ref,
    rows_ref,
    cot_ref,
    route_ref,
    router_ref,
    place_ref,
    w_in_ref,
    w_out_ref,
    act_ref,
    grad_pre_ref,
    x_ref,
    g_ref,
    ret_ref,
    back_a,
    back_b,
    gate_ref,
    produced,
    grad_rows,
    *,
    experts,
):
    ff, expert = pl.program_id(0), pl.program_id(1)
    slots = x_ref.shape[0]
    capacity = slots // full_ref.shape[1]
    half = capacity // 2

    @pl.when((ff == 0) & (expert == 0))
    def _():
        produced[...] = jnp.zeros_like(produced)
        grad_rows[...] = jnp.zeros_like(grad_rows)
        second = rows_ref[...]
        _, _, gate = routed_gate(second, router_ref[...], column_of(route_ref[...]), experts)
        gated = (gate * cot_ref[...].astype(F32)).astype(BF16)

        def pack(start):
            part = slice(start, start + half)
            slot = start + lax.broadcasted_iota(jnp.int32, (half, second.shape[0]), 0)
            pick = jnp.where(slot == place_ref[...], 1.0, 0.0).astype(BF16)
            x_ref[part, :] = dot(pick, second).astype(BF16)
            g_ref[part, :] = dot(pick, gated).astype(BF16)

        for owner in range(slots // capacity):
            pack(owner * capacity)
            pl.when(full_ref[0, owner] == 1)(
                functools.partial(pack, owner * capacity + half)
            )

    def run(rows):
        part = pl.ds(pl.multiple_of(expert * capacity, capacity), rows)
        pre = dot(x_ref[part, :], w_in_ref[0])
        grad_act = dot(g_ref[part, :], w_out_ref[0], NT)
        square = pre * pre
        bend = jnp.tanh(pre * (GELU_C + GELU_C * GELU_A * square))
        upper = 0.5 + 0.5 * bend
        act = (pre * upper).astype(BF16)
        inner = pre * (GELU_C + 3.0 * GELU_C * GELU_A * square)
        slope = upper + inner * (0.5 - 0.5 * bend * bend)
        grad_pre = (grad_act * slope).astype(BF16)
        act_ref[part, :] = act
        grad_pre_ref[part, :] = grad_pre
        produced[part, :] += dot(act, w_out_ref[0])
        grad_rows[part, :] += dot(grad_pre, w_in_ref[0], NT)

    on_rows(full_ref[0, expert], run, capacity)

    @pl.when((ff == pl.num_programs(0) - 1) & (expert == pl.num_programs(1) - 1))
    def _():
        count = ret_ref.shape[0]
        slot = lax.broadcasted_iota(jnp.int32, (count, slots), 1)
        place_col = column_of(place_ref[...])[:, :1]
        pick = jnp.where(slot == place_col, 1.0, 0.0).astype(BF16)
        returned = dot(pick, produced[...].astype(BF16))
        ret_ref[...] = returned.astype(BF16)
        grads = grad_rows[...].astype(BF16)
        back_a[...] = dot(pick[: count // 2], grads).astype(BF16)
        back_b[...] = dot(pick[count // 2 :], grads).astype(BF16)
        inner = jnp.sum(cot_ref[...].astype(F32) * returned, axis=1, keepdims=True)
        gate_ref[...] = jnp.broadcast_to(inner, (count, LANES)).T[:8]


def expert_rows(full, rows, cot, route_row, router, place, w_in, w_out, capacity, experts, ff_block):
    count, width = cot.shape
    local, _, ff = w_in.shape
    slots = local * capacity
    column = lambda f, e, _: (0, f)
    return pl.pallas_call(
        functools.partial(expert_kernel, experts=experts),
        grid_spec=pltpu.PrefetchScalarGridSpec(
            num_scalar_prefetch=1,
            grid=(ff // ff_block, local),
            in_specs=[
                whole_spec((count, width)),
                whole_spec((count, width)),
                whole_spec((1, count)),
                pl.BlockSpec((width, LANES), lambda *_: (0, width // LANES)),
                whole_spec((1, count)),
                pl.BlockSpec((1, width, ff_block), lambda f, e, _: (e, 0, f)),
                pl.BlockSpec((1, ff_block, width), lambda f, e, _: (e, f, 0)),
            ],
            out_specs=[
                pl.BlockSpec((slots, ff_block), column),
                pl.BlockSpec((slots, ff_block), column),
                whole_spec((slots, width)),
                whole_spec((slots, width)),
                whole_spec((count, width)),
                whole_spec((count // 2, width)),
                whole_spec((count // 2, width)),
                whole_spec((8, count)),
            ],
            scratch_shapes=[
                pltpu.VMEM((slots, width), F32),
                pltpu.VMEM((slots, width), F32),
            ],
        ),
        out_shape=[
            jax.ShapeDtypeStruct((slots, ff), BF16),
            jax.ShapeDtypeStruct((slots, ff), BF16),
            jax.ShapeDtypeStruct((slots, width), BF16),
            jax.ShapeDtypeStruct((slots, width), BF16),
            jax.ShapeDtypeStruct((count, width), BF16),
            jax.ShapeDtypeStruct((count // 2, width), BF16),
            jax.ShapeDtypeStruct((count // 2, width), BF16),
            jax.ShapeDtypeStruct((8, count), F32),
        ],
        compiler_params=params(),
        cost_estimate=lasting(28),
        name="expert_rows",
    )(full, rows, cot, route_row, router, place[None, :], w_in, w_out)


def weight_grad_kernel(full_ref, expert_ref, left_a, left_b, right_a, right_b, early_ref, late_ref):
    expert = expert_ref[0]
    capacity = left_a.shape[0]

    def run(rows_a, rows_b):
        total = (
            dot(left_a[:rows_a, :], right_a[:rows_a, :], TN)
            + dot(left_b[:rows_b, :], right_b[:rows_b, :], TN)
        ).astype(BF16)
        early_ref[0] = total[: early_ref.shape[1]]
        late_ref[0] = total[early_ref.shape[1] :]

    for full_a in range(2):
        for full_b in range(2):
            pl.when((full_ref[0, expert] == full_a) & (full_ref[1, expert] == full_b))(
                functools.partial(
                    run, capacity // (2 - full_a), capacity // (2 - full_b)
                )
            )


def early_rows(rows):
    return rows // 3 * 2


def weight_grad(full, expert, left, right, capacity, ff_block):
    slots, width = left[0].shape
    ff = max(width, right[0].shape[1])
    spec = lambda value: (
        pl.BlockSpec((capacity, ff_block), lambda f, _, e: (e[0], f))
        if value.shape[1] == ff
        else pl.BlockSpec(
            (capacity, value.shape[1]), lambda f, _, e: (e[0], 0), pipeline_mode=pl.Buffered(1)
        )
    )
    block = lambda value: ff_block if value.shape[1] == ff else value.shape[1]
    shape = (block(left[0]), block(right[0]))
    counts = (early_rows(shape[0]), shape[0] - early_rows(shape[0]))
    return pl.pallas_call(
        weight_grad_kernel,
        grid_spec=pltpu.PrefetchScalarGridSpec(
            num_scalar_prefetch=2,
            grid=(ff // ff_block,),
            in_specs=[spec(value) for value in (*left, *right)],
            out_specs=[
                pl.BlockSpec((1, count, shape[1]), lambda f, *_: (f, 0, 0)) for count in counts
            ],
        ),
        out_shape=[
            jax.ShapeDtypeStruct((ff // ff_block, count, shape[1]), BF16) for count in counts
        ],
        compiler_params=params(),
        cost_estimate=lasting(9),
        name="weight_grad",
    )(full, expert, *left, *right)


def hidden_back_kernel(
    bit_ref,
    own_a,
    own_b,
    sent_a,
    sent_b,
    hidden_ref,
    second_ref,
    att_ref,
    cot_ref,
    own_gate,
    sent_gate,
    route_ref,
    router_ref,
    w_ref,
    gain_ref,
    grad_hidden_ref,
    grad_att_ref,
    aug_ref,
    gate_out_ref,
    router_grad_ref,
    gain_grad_ref,
    keep_ref,
    give_ref,
    total,
    *,
    experts,
):
    step, steps = pl.program_id(0), pl.num_programs(0)

    @pl.when(step == 0)
    def _():
        router_grad_ref[...] = jnp.zeros_like(router_grad_ref)
        gain_grad_ref[...] = jnp.zeros_like(gain_grad_ref)
        total[...] = jnp.zeros_like(total)

    early = step < steps // 2
    of = lambda low, high: jnp.where(early, low[...], high[...])
    hidden, second, attended = hidden_ref[...], second_ref[...], att_ref[...]
    cot = cot_ref[...].astype(F32)
    scale = lax.rsqrt(jnp.mean(hidden * hidden, axis=1, keepdims=True) + EPSILON)
    probs, chosen, gate = routed_gate(
        second, router_ref[...], column_of(route_ref[...]), experts
    )
    inner = own_gate[0:1, :] + sent_gate[0:1, :]
    inner = jnp.broadcast_to(inner, (LANES, inner.shape[1])).T
    gate_out_ref[...] = jnp.broadcast_to(gate, gate_out_ref.shape)
    grad_logits = (probs * (jnp.where(chosen, inner, 0.0) - gate * inner)).astype(BF16)
    router_grad_ref[...] += dot(grad_logits, second, TN)
    grad_second = of(own_a, own_b).astype(F32) + of(sent_a, sent_b).astype(F32)
    grad_second = grad_second + dot(grad_logits, router_ref[...], NT)
    scaled_hidden = hidden * scale
    gain_grad_ref[...] += jnp.sum(grad_second * scaled_hidden, axis=0, keepdims=True)
    scaled = grad_second * gain_ref[...]
    mean = jnp.mean(scaled * scaled_hidden, axis=1, keepdims=True)
    grad_hidden = cot + scale * (scaled - scaled_hidden * mean)
    branch = grad_hidden.astype(BF16)
    grad_hidden_ref[...] = grad_hidden
    grad_att = dot(branch, w_ref[...], NT).astype(BF16)
    grad_att_ref[...] = grad_att
    total[...] += dot(attended, branch, TN)
    product = grad_att.astype(F32) * attended.astype(F32)
    rows, width = product.shape
    feature = lax.broadcasted_iota(jnp.int32, (width, LANES), 0)
    lane = lax.broadcasted_iota(jnp.int32, (width, LANES), 1)
    head = (lane & 15) == feature // 64
    collect = jnp.where(head & (lane < 48), 1.0, 0.0).astype(BF16)
    high = product.astype(BF16)
    rest = product - high.astype(F32)
    middle = rest.astype(BF16)
    low = (rest - middle.astype(F32)).astype(BF16)
    stats = dot(high, collect) + dot(middle, collect) + dot(low, collect)
    row_lane = lax.broadcasted_iota(jnp.int32, (rows, LANES), 1)
    aug_ref[...] = jnp.where(row_lane < 48, lane_parts(stats, row_lane), 0.0).astype(BF16)

    @pl.when(step == steps - 1)
    def _():
        keep_and_give(bit_ref[0], total[...], keep_ref, give_ref)


def hidden_back(bit, hidden, second, own, sent, att, cot, gates, route_row, out_full, gain, shards, experts, block=256):
    rows, width = cot.shape
    steps = rows // block
    half = steps // 2
    part = width // shards // 2
    here = lambda i, _: (i, 0)
    wide = lambda index: pl.BlockSpec((block, width), index)
    low = wide(lambda i, _: (jnp.minimum(i, half - 1), 0))
    high = wide(lambda i, _: (jnp.maximum(i - half, 0), 0))
    along = lambda height: pl.BlockSpec((height, block), lambda i, _: (0, i))
    return pl.pallas_call(
        functools.partial(hidden_back_kernel, experts=experts),
        grid_spec=pltpu.PrefetchScalarGridSpec(
            num_scalar_prefetch=1,
            grid=(steps,),
            in_specs=[low, high] * 2
            + [wide(here)] * 4
            + [
                along(8),
                along(8),
                along(1),
                pl.BlockSpec((width, LANES), lambda *_: (0, width // LANES)),
                pl.BlockSpec((width, width), lambda *_: (0, 0)),
                whole_spec((1, width)),
            ],
            out_specs=[
                wide(here),
                wide(here),
                pl.BlockSpec((block, LANES), here),
                pl.BlockSpec((block, LANES), here),
                whole_spec((LANES, width)),
                whole_spec((1, width)),
                whole_spec((shards, part, width)),
                whole_spec((shards, part, width)),
            ],
            scratch_shapes=[pltpu.VMEM((width, width), F32)],
        ),
        out_shape=[
            jax.ShapeDtypeStruct((rows, width), F32),
            jax.ShapeDtypeStruct((rows, width), BF16),
            jax.ShapeDtypeStruct((rows, LANES), BF16),
            jax.ShapeDtypeStruct((rows, LANES), F32),
            jax.ShapeDtypeStruct((LANES, width), F32),
            jax.ShapeDtypeStruct((1, width), F32),
            jax.ShapeDtypeStruct((shards, part, width), BF16),
            jax.ShapeDtypeStruct((shards, part, width), BF16),
        ],
        compiler_params=params(),
        cost_estimate=lasting(12),
        name="hidden_back",
    )(bit, *own, *sent, hidden, second, att, cot, *gates, route_row, out_full, out_full, gain)


def token_back_kernel(tok_ref, grad_ref, gain_ref, *refs):
    weights, triples, out_ref = refs[:GATHERS], refs[GATHERS:-1], refs[-1]
    rows = tok_ref[...].astype(F32)
    scale = lax.rsqrt(jnp.mean(rows * rows, axis=1, keepdims=True) + EPSILON)
    grads = jnp.concatenate([t[p] for p in range(3) for t in triples], axis=1)
    span = grads.shape[1] // len(weights)
    grad_normed = jnp.zeros(rows.shape, F32)
    for at, weight in enumerate(weights):
        grad_normed += dot(grads[:, at * span : (at + 1) * span], weight[...], NT)
    scaled_rows = rows * scale
    scaled = grad_normed * gain_ref[...]
    mean = jnp.mean(scaled * scaled_rows, axis=1, keepdims=True)
    out_ref[...] = (grad_ref[...] + scale * (scaled - scaled_rows * mean)).astype(BF16)


def token_back(tokens, grad_hidden, grad_triples, weights, gain_row, block=256):
    rows, width = tokens.shape
    here = lambda i: (i, 0)
    return pl.pallas_call(
        token_back_kernel,
        grid=(rows // block,),
        in_specs=[
            pl.BlockSpec((block, width), here),
            pl.BlockSpec((block, width), here),
            whole_spec((1, width)),
        ]
        + [whole_spec((width, 3 * width // len(weights))) for w in weights]
        + [pl.BlockSpec((3, block, t.shape[2]), lambda i: (0, i, 0)) for t in grad_triples],
        out_specs=pl.BlockSpec((block, width), here),
        out_shape=jax.ShapeDtypeStruct((rows, width), BF16),
        compiler_params=params(),
        cost_estimate=lasting(9),
        name="token_back",
    )(tokens, grad_hidden, gain_row, *weights, *grad_triples)


def swap(value, axis, step=1):
    size = lax.axis_size(axis)
    return lax.ppermute(value, axis, [(i, i ^ step) for i in range(size)])


def bit_of(axis, step):
    return lax.axis_index(axis) // step % 2


def bits(size, first=1):
    return [1 << n for n in range(first.bit_length() - 1, size.bit_length() - 1)]


def rounded(parts):
    return sum(part.astype(F32) for part in parts).astype(BF16)


def exchange(parts, axis, step, pick):
    bit = bit_of(axis, step)
    give = rounded([pick(part, 1 - bit) for part in parts])
    return [pick(part, bit) for part in parts] + [swap(give, axis, step)]


def halve(parts, axis, step):
    def pick(part, bit):
        parted = part.reshape((part.shape[0], 2, part.shape[1] // 2) + part.shape[2:])
        return lax.dynamic_index_in_dim(parted, bit, 1, keepdims=False)

    return exchange(parts, axis, step, pick)


def to_owner(parts, steps):
    def pick(part, bit):
        parted = part.reshape((part.shape[0] // 2, 2) + part.shape[1:])
        return lax.dynamic_index_in_dim(parted, bit, 1, keepdims=False)

    for step in steps:
        parts = exchange(parts, "shard", step, pick)
    return parts


def to_owner_early(parts):
    return to_owner(parts, bits(lax.axis_size("shard"))[:-1])


def to_owner_last(parts):
    return to_owner(parts, bits(lax.axis_size("shard"))[-1:])


def both(parts, axis, step):
    mine = rounded(parts)
    return [mine, swap(mine, axis, step)]


def unhalve(value, axis, step, dim):
    other = swap(value, axis, step)
    first = bit_of(axis, step) == 0
    low = jnp.where(first, value, other)
    high = jnp.where(first, other, value)
    return jnp.concatenate([low, high], axis=dim)


def neighbours(parts):
    return halve(parts, "dp", 1) if lax.axis_size("dp") > 1 else parts


def spread(parts):
    for step in bits(lax.axis_size("dp"), 2):
        parts = halve(parts, "dp", step)
    return parts


def unspread(value):
    for step in reversed(bits(lax.axis_size("dp"), 2)):
        value = unhalve(value, "dp", step, 0)
    return value


def summed(parts):
    for step in bits(lax.axis_size("dp"), 2):
        parts = both(parts, "dp", step)
    return parts


def finish_expert(early, late, local):
    early, late = rounded(early)[0], rounded(late)[0]
    whole = jnp.concatenate([unspread(early), rounded(summed([late]))], axis=0)
    if lax.axis_size("dp") > 1:
        whole = unhalve(whole, "dp", 1, 0)
    return whole.reshape((local, -1) + whole.shape[1:]).astype(F32)


def tie(value, *sums):
    value, *last = lax.optimization_barrier((value,) + tuple(parts[-1] for parts in sums))
    return (value, *(parts[:-1] + [part] for parts, part in zip(sums, last)))


def dense_across(parts):
    return halve(parts, "expert", 1) if lax.axis_size("expert") > 1 else parts


def dense_finish(parts):
    parts = [rounded(parts)[0]]
    for axis in ("expert", "dp"):
        for step in bits(lax.axis_size(axis), 2):
            parts = both(parts, axis, step)
    value = rounded(parts)
    for axis in ("expert", "dp"):
        if lax.axis_size(axis) > 1:
            value = unhalve(value, axis, 1, 0)
    return value.astype(F32)


def gather_far(value):
    shards, parts = lax.axis_size("shard"), lax.axis_size("dp")
    rows, columns = value.shape
    parted = value.reshape(parts, rows // parts, columns)
    mine = lax.dynamic_index_in_dim(parted, lax.axis_index("dp"), 0, keepdims=False)
    me = lax.axis_index("shard")
    whole = lax.dynamic_update_index_in_dim(
        jnp.zeros((shards,) + mine.shape, value.dtype), mine, me, 0
    )
    for away in range(1, shards):
        piece = lax.ppermute(mine, "shard", [(i, (i + away) % shards) for i in range(shards)])
        whole = lax.dynamic_update_index_in_dim(whole, piece, (me - away) % shards, 0)
    return whole


def gather_near(share):
    shards, rows, columns = share.shape
    whole = share[:, None]
    for step in reversed(bits(lax.axis_size("dp"))):
        other = swap(whole, "dp", step)
        first = bit_of("dp", step) == 0
        low, high = jnp.where(first, whole, other), jnp.where(first, other, whole)
        whole = jnp.stack([low, high], axis=2)
        whole = whole.reshape(shards, -1, rows, columns)
    return whole.reshape(-1, columns)


def places_of(route_ids, first, local, capacity):
    owned = route_ids - first
    choose = owned[:, None] == jnp.arange(local, dtype=jnp.int32)[None, :]
    rank = jnp.cumsum(choose.astype(jnp.int32), axis=0) - 1
    slot = jnp.sum(jnp.where(choose, rank, 0), axis=1) + owned * capacity
    full = (rank[-1] >= capacity // 2).astype(jnp.int32)
    return jnp.where(jnp.any(choose, axis=1), slot, -1), full


def experts_of_pairs(second, cotangent, routes, out_full, expert_in, expert_out, experts, early):
    rows, width = cotangent.shape
    local, _, ff = expert_in.shape
    capacity = 2 * rows // experts
    ff_block = ff // lax.axis_size("shard")
    other_cot, other_routes = early
    other_second = swap(second, "expert")
    first_own = lax.axis_index("expert") * local
    results, flags = [], []
    for rows_of, cot, route_ids in (
        (second, cotangent, routes),
        (other_second, other_cot, other_routes),
    ):
        place, full = places_of(route_ids, first_own, local, capacity)
        if results:
            rows_of, _ = lax.optimization_barrier((rows_of, results[0][7]))
        results.append(
            expert_rows(
                full[None],
                rows_of,
                cot,
                route_ids[None, :],
                out_full,
                place,
                expert_in,
                expert_out,
                capacity,
                experts,
                ff_block,
            )
        )
        flags.append(full)
    own, other = results
    full = jnp.stack(flags)
    keep = bit_of("dp", 1)
    one = lambda expert: expert[None].astype(jnp.int32)
    grad = lambda expert, left, right: weight_grad(
        full, one(expert), left, right, capacity, ff_block
    )
    acts, grads = (own[0], other[0]), (own[3], other[3])
    xs, grad_pres = (own[2], other[2]), (own[1], other[1])
    back_a = swap(other[5], "expert")
    sent_gate = swap(other[7], "expert")
    out_give = grad(1 - keep, acts, grads)
    full, *out_give = lax.optimization_barrier((full, *out_give))
    out_keep = grad(keep, acts, grads)
    full, back_a, sent_gate, back_b, *out_both = lax.optimization_barrier(
        (full, back_a, sent_gate, other[6], *out_keep, *out_give)
    )
    back_b = swap(back_b, "expert")
    out_keep, out_sent = out_both[:2], [swap(part, "dp") for part in out_both[2:]]
    in_give = grad(1 - keep, xs, grad_pres)
    full, *out_sent = lax.optimization_barrier((full, *out_sent, *in_give))
    out_sent, in_give = out_sent[:2], out_sent[2:]
    in_sent = [swap(part, "dp") for part in in_give]
    out_early = spread([out_keep[0], out_sent[0]])
    out_late = to_owner_early([out_keep[1], out_sent[1]])
    in_keep = grad(keep, xs, grad_pres)
    gate, *in_keep = lax.optimization_barrier((own[7], *in_keep))
    in_near = tuple([mine, sent] for mine, sent in zip(in_keep, in_sent))
    return (own[4], other[4]), (own[5:7], (back_a, back_b)), (gate, sent_gate), in_near, (out_early, out_late)


def experts_of_many(second, cotangent, route_ids, router, expert_in, expert_out):
    tok_rows, width = second.shape
    experts_all = router.shape[1]
    local, _, ff = expert_in.shape
    groups = lax.axis_size("expert")
    shards = lax.axis_size("shard")
    capacity = 2 * tok_rows // experts_all
    choose = route_ids[:, None] == jnp.arange(experts_all, dtype=jnp.int32)[None, :]
    rank = jnp.cumsum(choose.astype(jnp.int32), axis=0) - 1
    slot_index = route_ids * capacity + jnp.sum(jnp.where(choose, rank, 0), axis=1)
    probs = jax.nn.softmax(dot(second, router), axis=-1)
    gate = jnp.sum(jnp.where(choose, probs, 0.0), axis=1)

    def across(value):
        return lax.all_to_all(value, "expert", split_axis=0, concat_axis=0, tiled=True)

    def to_slots(token_rows):
        filled = jnp.zeros((experts_all * capacity, width), token_rows.dtype)
        filled = filled.at[slot_index].set(token_rows)
        return across(filled.reshape(groups, local, capacity, width))

    def from_slots(value):
        return across(value).reshape(experts_all * capacity, width)[slot_index]

    def einsum(form, left, right):
        return jnp.einsum(form, left, right, preferred_element_type=F32)

    def gelu(value):
        return jax.nn.gelu(value, approximate=True)

    grad_out = cotangent.astype(F32)
    arrived = to_slots(second)
    pre_act, pull = jax.vjp(gelu, einsum("aecd,edf->aecf", arrived, expert_in))
    activated = pre_act.astype(BF16)
    produced = einsum("aecf,efd->aecd", activated, expert_out).astype(BF16)
    returned = from_slots(produced)
    inner = jnp.sum(grad_out * returned.astype(F32), axis=1)
    grad_arrived = to_slots((gate[:, None] * grad_out).astype(BF16))
    grad_act = einsum("aecd,efd->aecf", grad_arrived, expert_out)
    grad_pre = pull(grad_act)[0].astype(BF16)
    grad_w_out = einsum("aecf,aecd->efd", activated, grad_arrived).astype(BF16)
    grad_w_in = einsum("aecd,aecf->edf", arrived, grad_pre).astype(BF16)
    back = from_slots(einsum("aecf,edf->aecd", grad_pre, expert_in).astype(BF16))
    grad_w_in = grad_w_in.reshape(local, width, shards, ff // shards).transpose(2, 0, 1, 3)
    grad_w_out = grad_w_out.reshape(local, shards, ff // shards, width).transpose(1, 0, 2, 3)
    def near(value):
        parts = neighbours([value.reshape((shards, -1) + value.shape[3:])])
        cut = early_rows(parts[0].shape[1])
        return [part[:, :cut] for part in parts], [part[:, cut:] for part in parts]

    out_early, out_late = near(grad_w_out)
    back = jnp.split(back, 2, axis=0)
    nothing = [jnp.zeros_like(part) for part in back]
    inner = jnp.broadcast_to(inner[None, :], (8, tok_rows))
    return (
        (returned, jnp.zeros_like(returned)),
        (back, nothing),
        (inner, jnp.zeros_like(inner)),
        near(grad_w_in),
        (spread(out_early), to_owner_early(out_late)),
    )


def body(
    tokens,
    segments,
    routes,
    cotangent,
    attn_in,
    attn_out,
    router,
    gain_one,
    gain_two,
    expert_in,
    expert_out,
):
    rows, width = tokens.shape
    experts = router.shape[1]
    local = expert_in.shape[0]
    lanes_of = lambda value: jnp.pad(value[:, None], ((0, 0), (0, LANES - 1)))
    padded = lambda value: jnp.pad(value, ((0, 0), (0, LANES - experts)))
    segment_col = segments[0][:, None]
    route_ids = routes.reshape(rows)
    bit = bit_of("dp", 1)[None].astype(jnp.int32)
    shards = lax.axis_size("shard")
    pairs_only = lax.axis_size("expert") == local == 2
    early = None

    span = 3 * width // GATHERS
    pieces = [attn_in[:, g * span : (g + 1) * span] for g in range(GATHERS)]
    pieces[0] = jnp.concatenate([pieces[0], lanes_of(gain_one)], axis=1)
    shares = [gather_far(piece) for piece in pieces]
    source = jnp.concatenate([attn_out, padded(router), lanes_of(gain_two)], axis=1)
    weights = [gather_near(share) for share in shares]
    source, *weights = lax.optimization_barrier((source, *weights))
    first_gain = weights[0][:, span].astype(F32)[None, :]
    if pairs_only:
        early = (swap(cotangent, "expert"), swap(route_ids, "expert"))
    share = gather_far(source)

    normed, triple = qkv(tokens, first_gain, weights, span)
    triple, share = lax.optimization_barrier((triple, share))
    out_full = gather_near(share)
    second_gain = out_full[:, width + LANES].astype(F32)[None, :]
    attended, qaug = attend_forward(triple, segment_col)
    hidden, second = project(tokens, attended, out_full, second_gain)
    if pairs_only:
        done = experts_of_pairs(
            second, cotangent, route_ids, out_full, expert_in, expert_out, experts, early
        )
    else:
        full_router = out_full[:, width : width + experts]
        done = experts_of_many(
            second, cotangent, route_ids, full_router, expert_in, expert_out
        )
    returned, (own_back, sent_back), inner, in_near, (out_early, out_late) = done

    in_early, in_late = in_near
    gate, out_late, in_early, in_late = tie(inner[0], out_late, in_early, in_late)
    out_late = to_owner_last(out_late)
    in_late = to_owner_early(in_late)
    (
        grad_hidden,
        grad_att,
        gaug,
        gates,
        grad_router,
        grad_gain_two,
        keep_out,
        give_out,
    ) = hidden_back(
        bit,
        hidden,
        second,
        own_back,
        sent_back,
        attended,
        cotangent,
        (gate, inner[1]),
        route_ids[None, :],
        out_full,
        second_gain,
        shards,
        experts,
    )
    heads = width // 64 // GROUPS
    back = lambda grad, g: attend_backward(
        bit, triple, grad, segment_col, qaug, gaug, normed, shards, g * heads, heads
    )

    grad_att, out_early, (made,) = tie(grad_att, out_early, [returned[1]])
    made = swap(made, "expert") if pairs_only else made
    out_early = to_owner_early(out_early)
    in_early = spread(in_early)
    grads_0, keep_0, give_0 = back(grad_att, 0)
    small = padded(grad_router[:experts].T.astype(BF16))
    small = jnp.concatenate([small, lanes_of(grad_gain_two[0].astype(BF16))], axis=1)
    small = small.reshape(shards, 2, width // shards // 2, 2 * LANES)
    pick = lambda half: lax.dynamic_index_in_dim(small, half, 1, keepdims=False)
    keep_a = jnp.concatenate([keep_out, pick(bit[0]), keep_0], axis=2)
    give_a = jnp.concatenate([give_out, pick(1 - bit[0]), give_0], axis=2)
    dense_a = [keep_a, swap(give_a, "dp")]

    grad_att, out_early, out_late, in_late, (grads_0,) = tie(
        grad_att, out_early, out_late, in_late, [grads_0]
    )
    out_early = to_owner_last(out_early)
    in_late = to_owner_last(in_late)
    grads_1, keep_1, give_1 = back(grad_att, 1)

    grad_att, in_early, dense_a, (grads_1,) = tie(grad_att, in_early, dense_a, [grads_1])
    in_early = to_owner_early(in_early)
    dense_a = dense_across(dense_a)
    grads_2, keep_2, give_2 = back(grad_att, 2)
    keep_b = jnp.concatenate([keep_1, keep_2], axis=2)
    dense_b = [keep_b, swap(jnp.concatenate([give_1, give_2], axis=2), "dp")]

    grad_hidden, in_early, out_early, in_late, dense_a, (grads_2,) = tie(
        grad_hidden, in_early, out_early, in_late, dense_a, [grads_2]
    )
    in_early = to_owner_last(in_early)
    final_out = finish_expert(out_early, out_late, local)
    dense_a = to_owner_early(dense_a)
    grad_tokens = token_back(
        tokens, grad_hidden, (grads_0, grads_1, grads_2), weights, first_gain
    )
    dense_b = dense_across(dense_b)
    dense_a = dense_finish(to_owner_last(dense_a))
    dense_b = dense_finish(to_owner_last(to_owner_early(dense_b)))
    final_in = finish_expert(in_early, in_late, local)

    start = width + 2 * LANES
    pair_columns = lambda value, start: [
        value[:, c : c + LANES] for c in range(start, value.shape[1], LANES)
    ]
    columns = pair_columns(dense_a, start) + pair_columns(dense_b, 0)
    grad_attn_in = jnp.concatenate(columns[0::3] + columns[1::3] + columns[2::3], axis=1)
    grad_gain_one = jnp.sum(attn_in.astype(F32) * grad_attn_in, axis=1) / gain_one.astype(F32)

    wide = returned[0].astype(F32) + made.astype(F32)
    layer = hidden + gates[:, :1] * wide
    return (
        layer.astype(BF16),
        grad_tokens,
        grad_attn_in,
        dense_a[:, :width],
        dense_a[:, width : width + experts],
        grad_gain_one,
        dense_a[:, width + LANES],
        final_in,
        final_out,
    )


def solution(mesh):
    everywhere = P(("dp", "expert", "shard"), None)
    placed = (everywhere,) * 4 + (P("shard", None),) * 3 + (P("shard"),) * 2
    placed = placed + (P("expert", None, None),) * 2
    outs = (everywhere,) * 2 + (P("shard", None),) * 3 + (P("shard"),) * 2
    outs = outs + (P("expert", None, "shard"), P("expert", "shard", None))
    return jax.shard_map(
        body, mesh=mesh, in_specs=placed, out_specs=outs, check_vma=False
    )
```

time: 559 us -> 475 us (0.85)
  local copies, waits for them, and re-layouts: 65.6 us -> 25.8 us
  waiting for transfers between devices: 109 us -> 74.5 us
  Pallas kernels: 207 us -> 223 us
  starting transfers between devices: 82.2 us -> 66.6 us
  matrix products: 11.8 us -> 0 us
  other arithmetic: 71.1 us -> 77.4 us
    ppermute x46 -> x47, waiting for transfers between devices: 102 us -> 58.2 us  [swap(): return lax.ppermute(value, axis, [(i, i ^ step) for i in range(size)])]
    slice x14 -> x1, local copies, waits for them, and re-layouts: 21.1 us -> 0.2 us  [body(): layer = hidden + gates[:, :1] * wide]
    ppermute x46 -> x47, starting transfers between devices: 70.5 us -> 57.1 us  [swap(): return lax.ppermute(value, axis, [(i, i ^ step) for i in range(size)])]
    pallas_call x2, Pallas kernels: 63.8 us -> 76.9 us  [expert_rows(): pl.pallas_call(functools.partial(expert_kernel, experts=experts), grid_sp...]
    dot_general x4 -> x0, matrix products: 11.8 us -> none  [the longest x3 7.39 us: body(): jnp.einsum('td,pte->dpe', normed, grads, preferred_element_type=F32)]
    ppermute x9, waiting for transfers between devices: 6.79 us -> 16.4 us  [gather_far(): lax.ppermute(mine, 'shard', [(i, (i + away) % shards) for i in range(shar...]
    convert_element_type x20, other arithmetic: 26.3 us -> 34 us  [rounded(): return sum((part.astype(F32) for part in parts)).astype(BF16)]
    pallas_call x2 -> x1, Pallas kernels: 29.3 us -> 21.8 us  [attend_forward(): pl.pallas_call(functools.partial(attend_kernel, block=block), grid=(pairs...]
  transfers between devices with their start and end apart: 55 -> 56, of which waited for: 17 -> 15; matrix products, arithmetic and copies ran while one was open for 25% -> 20% of each run, Pallas kernels for 30% -> 40%
where the time goes in v2:
time: 475 us; the launch traced here: 469 us
  Pallas kernels  223 us (47%)
  other arithmetic  77.4 us (16%)
  waiting for transfers between devices  74.5 us (16%)
  starting transfers between devices  66.6 us (14%)
  local copies, waits for them, and re-layouts  25.8 us (5%)
    pallas_call x2, Pallas kernels, expert_rows(): pl.pallas_call(functools.partial(expert_kernel, experts=experts), grid_sp...  76.9 us
    ppermute x47, waiting for transfers between devices, swap(): return lax.ppermute(value, axis, [(i, i ^ step) for i in range(size)])  58.2 us
    ppermute x47, starting transfers between devices, swap(): return lax.ppermute(value, axis, [(i, i ^ step) for i in range(size)])  57.1 us
    pallas_call x3, Pallas kernels, attend_backward(): pl.pallas_call(functools.partial(attend_back_kernel, block=block, first_h...  47.9 us
    pallas_call x4, Pallas kernels, weight_grad(): pl.pallas_call(weight_grad_kernel, grid_spec=pltpu.PrefetchScalarGridSpec...  38.6 us
    convert_element_type x20, other arithmetic, rounded(): return sum((part.astype(F32) for part in parts)).astype(BF16)  34 us
    pallas_call x1, Pallas kernels, attend_forward(): pl.pallas_call(functools.partial(attend_kernel, block=block), grid=(pairs...  21.8 us
    ppermute x9, waiting for transfers between devices, gather_far(): lax.ppermute(mine, 'shard', [(i, (i + away) % shards) for i in range(shar...  16.4 us
  transfers between devices with their start and end apart: 56, of which 15 were waited for; matrix products, arithmetic and copies ran while one was open for 20% of the time, Pallas kernels for 40%

profile of v2, /device:TPU:1, one launch (start us, length us, event | category | flops | bytes accessed | tf_op | source)
XLA Modules:
  0.0 469.4 jit_solution(10579417474387492714)
XLA Ops:
  9.4 8.3 %collective-permute-done.5 = bf16[48,1152]{1,0:T(8,128)(2,1)S(1)} collective-permute-done((bf16[48,1152]{1,0:T(8,128)(2,1)S(1)}, bf16[48,1152]{1,0:T(8,128)(2,1)S(1)}, u32[]{:S(2)}, u32[]{:S(2)}) %collective-permute-start.5) | collective-permute-done | bytes 110624 | tf_op jit(solution)/shard_map/ppermute | solution.py:784
  17.7 8.0 %collective-permute-done.6 = bf16[48,1152]{1,0:T(8,128)(2,1)S(1)} collective-permute-done((bf16[48,1152]{1,0:T(8,128)(2,1)S(1)}, bf16[48,1152]{1,0:T(8,128)(2,1)S(1)}, u32[]{:S(2)}, u32[]{:S(2)}) %collective-permute-start.6) | collective-permute-done | bytes 110624 | tf_op jit(solution)/shard_map/ppermute | solution.py:784
  29.4 7.5 %collective-permute-done.8 = bf16[4,1,48,1152]{3,2,0,1:T(8,128)(2,1)S(1)} collective-permute-done((bf16[4,1,48,1152]{3,2,0,1:T(8,128)(2,1)S(1)}, bf16[4,1,48,1152]{3,2,0,1:T(8,128)(2,1)S(1)}, u32[]{:S(2)}, u32[]{:S(2)}) %collective-permute-start.8) | collective-permute-done | bytes 442400 | tf_op jit(solution)/shard_map/ppermute | solution.py:663
  37.1 6.7 %collective-permute-start.9 = (bf16[4,2,48,1152]{3,2,1,0:T(8,128)(2,1)S(1)}, bf16[4,2,48,1152]{3,2,1,0:T(8,128)(2,1)S(1)}, u32[]{:S(2)}, u32[]{:S(2)}) collective-permute-start(bf16[4,2,48,1152]{3,2,1,0:T(8,128)(2,1)S(1)} %maximum_bitcast_fusion.1), channel_id=1, source_target_pairs={{0,8},{8,0},{16,24},{24,16},{1,9},{9,1},{17,25},{25,17},{2,10},{10... | collective-permute-start | bytes 2654216 | tf_op jit(solution)/shard_map/ppermute | solution.py:663
  58.0 8.3 %qkv.1 = (bf16[1024,768]{1,0:T(8,128)(2,1)}, bf16[1024,2304]{1,0:T(8,128)(2,1)}) custom-call(bf16[1024,768]{1,0:T(8,128)(2,1)} %tok_ref.5, f32[1,768]{1,0:T(1,128)} %reshape.1062.gain_ref, bf16[768,1280]{1,0:T(8,128)(2,1)} %bitcast.280, bf16[768,1152]{1,0:T(8,128)(2,1)} %bitcast.282), custom_call_target="tpu_custom_call" | custom-call | flops 460000000 | tf_op jit(solution)/shard_map/qkv/pallas_call | solution.py:244
  69.7 6.2 %collective-permute-done.13 = bf16[4,1,48,1024]{3,2,0,1:T(8,128)(2,1)S(1)} collective-permute-done((bf16[4,1,48,1024]{3,2,0,1:T(8,128)(2,1)S(1)}, bf16[4,1,48,1024]{3,2,0,1:T(8,128)(2,1)S(1)}, u32[]{:S(2)}, u32[]{:S(2)}) %collective-permute-start.13) | collective-permute-done | bytes 393248 | tf_op jit(solution)/shard_map/ppermute | solution.py:663
  80.0 21.8 %attend_forward.1 = (bf16[1024,768]{1,0:T(8,128)(2,1)}, bf16[1024,128]{1,0:T(8,128)(2,1)}) custom-call(bf16[1024,2304]{1,0:T(8,128)(2,1)} %get-tuple-element.107.q_ref.k_ref.v_ref, bf16[1024,2304]{1,0:T(8,128)(2,1)} %get-tuple-element.107.q_ref.k_ref.v_ref, bf16[1024,2304]{1,0:T(8,128)(2,1)} %get-tuple-element.107.q_ref.k_ref.v_ref, s32[1024,1]{1,0:T(8,128)} %copy.140.seg_ref), custom_call_target="tpu_custom_call" | custom-call | flops 1380000000 | tf_op jit(solution)/shard_map/attend_forward/pallas_call | solution.py:106
  104.4 5.8 %project.1 = (f32[1024,768]{1,0:T(8,128)}, bf16[1024,768]{1,0:T(8,128)(2,1)}) custom-call(bf16[1024,768]{1,0:T(8,128)(2,1)} %tok_ref.5, bf16[1024,768]{1,0:T(8,128)(2,1)} %get-tuple-element.108.att_ref, bf16[768,1024]{1,0:T(8,128)(2,1)} %bitcast.274, f32[1,768]{1,0:T(1,128)} %reshape.1063.gain_ref), custom_call_target="tpu_custom_call" | custom-call | flops 402500000 | tf_op jit(solution)/shard_map/project/pallas_call | solution.py:273
  115.1 40.0 %expert_rows.2 = (bf16[1024,3072]{1,0:T(8,128)(2,1)}, bf16[1024,3072]{1,0:T(8,128)(2,1)}, bf16[1024,768]{1,0:T(8,128)(2,1)}, bf16[1024,768]{1,0:T(8,128)(2,1)}, ...) custom-call(s32[1,2]{1,0:T(1,128)} %compare_convert_fusion.1.full_ref, ...), custom_call_target="tpu_custom_call" | custom-call | flops 1610000000 | tf_op jit(solution)/shard_map/expert_rows/pallas_call | solution.py:390
  156.3 36.9 %expert_rows.3 = (bf16[1024,3072]{1,0:T(8,128)(2,1)}, bf16[1024,3072]{1,0:T(8,128)(2,1)}, bf16[1024,768]{1,0:T(8,128)(2,1)}, bf16[1024,768]{1,0:T(8,128)(2,1)}, ...) custom-call(s32[1,2]{1,0:T(1,128)} %compare_convert_fusion.full_ref, ...), custom_call_target="tpu_custom_call" | custom-call | flops 1610000000 | tf_op jit(solution)/shard_map/expert_rows/pallas_call | solution.py:390
  193.9 9.6 %weight_grad.4 = (bf16[4,512,768]{2,1,0:T(8,128)(2,1)}, bf16[4,256,768]{2,1,0:T(8,128)(2,1)}) custom-call(s32[2,2]{1,0:T(2,128)} %pad_add_fusion.full_ref, s32[1]{0:T(128)} %bitcast.59.expert_ref, bf16[1024,3072]{1,0:T(8,128)(2,1)} %get-tuple-element.114.left_a, bf16[1024,3072]{1,0:T(8,128)(2,1)} %get-tuple-element.117.left_b, ...), custom_call_target="tpu_custom_call" | custom-call | flops 517500000 | tf_op jit(solution)/shard_map/weight_grad/pallas_call | solution.py:473
  204.0 9.8 %weight_grad.5 = (bf16[4,512,768]{2,1,0:T(8,128)(2,1)}, bf16[4,256,768]{2,1,0:T(8,128)(2,1)}) custom-call(s32[2,2]{1,0:T(2,128)} %pad_add_fusion.full_ref, s32[1]{0:T(128)} %bitcast.47.expert_ref.bit_ref, bf16[1024,3072]{1,0:T(8,128)(2,1)} %get-tuple-element.114.left_a, bf16[1024,3072]{1,0:T(8,128)(2,1)} %get-tuple-element.117.left_b, ...), custom_call_target="tpu_custom_call" | custom-call | flops 517500000 | tf_op jit(solution)/shard_map/weight_grad/pallas_call | solution.py:473
  214.7 9.4 %weight_grad.6 = (bf16[4,512,768]{2,1,0:T(8,128)(2,1)}, bf16[4,256,768]{2,1,0:T(8,128)(2,1)}) custom-call(s32[2,2]{1,0:T(2,128)} %pad_add_fusion.full_ref, s32[1]{0:T(128)} %bitcast.59.expert_ref, bf16[1024,768]{1,0:T(8,128)(2,1)} %get-tuple-element.135.left_a, bf16[1024,768]{1,0:T(8,128)(2,1)} %get-tuple-element.136.left_b, ...), custom_call_target="tpu_custom_call" | custom-call | flops 517500000 | tf_op jit(solution)/shard_map/weight_grad/pallas_call | solution.py:473
  236.4 9.8 %weight_grad.7 = (bf16[4,512,768]{2,1,0:T(8,128)(2,1)}, bf16[4,256,768]{2,1,0:T(8,128)(2,1)}) custom-call(s32[2,2]{1,0:T(2,128)} %pad_add_fusion.full_ref, s32[1]{0:T(128)} %bitcast.47.expert_ref.bit_ref, bf16[1024,768]{1,0:T(8,128)(2,1)} %get-tuple-element.135.left_a, bf16[1024,768]{1,0:T(8,128)(2,1)} %get-tuple-element.136.left_b, ...), custom_call_target="tpu_custom_call" | custom-call | flops 517500000 | tf_op jit(solution)/shard_map/weight_grad/pallas_call | solution.py:473
  254.0 14.1 %hidden_back.1 = (f32[1024,768]{1,0:T(8,128)}, bf16[1024,768]{1,0:T(8,128)(2,1)}, bf16[1024,128]{1,0:T(8,128)(2,1)}, f32[1024,128]{1,0:T(8,128)}, f32[128,768]{1...) custom-call(s32[1]{0:T(128)} %bitcast.47.expert_ref.bit_ref, ...), custom_call_target="tpu_custom_call" | custom-call | flops 690000000 | tf_op jit(solution)/shard_map/hidden_back/pallas_call | solution.py:582
  284.4 15.8 %attend_backward.3 = (bf16[3,1024,256]{2,1,0:T(8,128)(2,1)}, bf16[4,96,768]{2,1,0:T(8,128)(2,1)}, bf16[4,96,768]{2,1,0:T(8,128)(2,1)}) custom-call(s32[1]{0:T(128)} %bitcast.47.expert_ref.bit_ref, bf16[1024,2304]{1,0:T(8,128)(2,1)} %get-tuple-element.107.q_ref.k_ref.v_ref, bf16[1024,2304]{1,0:T(8,128)(2,1)} %get-tuple-element.107.q_ref.k_ref.v_ref, ...), custom_call_target="tpu_custom_call" | custom-call | flops 805000000 | tf_op jit(solution)/shard_map/attend_backward/pallas_call | solution.py:199
  309.2 5.0 %collective-permute-done.30 = bf16[2,256,768]{2,1,0:T(8,128)(2,1)} collective-permute-done((bf16[2,256,768]{2,1,0:T(8,128)(2,1)}, bf16[2,256,768]{2,1,0:T(8,128)(2,1)}, u32[]{:S(2)}, u32[]{:S(2)}) %collective-permute-start.30) | collective-permute-done | bytes 786464 | tf_op jit(solution)/shard_map/ppermute | solution.py:663
  320.0 16.1 %attend_backward.4 = (bf16[3,1024,256]{2,1,0:T(8,128)(2,1)}, bf16[4,96,768]{2,1,0:T(8,128)(2,1)}, bf16[4,96,768]{2,1,0:T(8,128)(2,1)}) custom-call(s32[1]{0:T(128)} %bitcast.47.expert_ref.bit_ref, bf16[1024,2304]{1,0:T(8,128)(2,1)} %get-tuple-element.107.q_ref.k_ref.v_ref, bf16[1024,2304]{1,0:T(8,128)(2,1)} %get-tuple-element.107.q_ref.k_ref.v_ref, ...), custom_call_target="tpu_custom_call" | custom-call | flops 805000000 | tf_op jit(solution)/shard_map/attend_backward/pallas_call | solution.py:199
  346.8 16.0 %attend_backward.5 = (bf16[3,1024,256]{2,1,0:T(8,128)(2,1)}, bf16[4,96,768]{2,1,0:T(8,128)(2,1)}, bf16[4,96,768]{2,1,0:T(8,128)(2,1)}) custom-call(s32[1]{0:T(128)} %bitcast.47.expert_ref.bit_ref, bf16[1024,2304]{1,0:T(8,128)(2,1)} %get-tuple-element.107.q_ref.k_ref.v_ref, bf16[1024,2304]{1,0:T(8,128)(2,1)} %get-tuple-element.107.q_ref.k_ref.v_ref, ...), custom_call_target="tpu_custom_call" | custom-call | flops 805000000 | tf_op jit(solution)/shard_map/attend_backward/pallas_call | solution.py:199
  385.7 9.5 %token_back.1 = bf16[1024,768]{1,0:T(8,128)(2,1)} custom-call(bf16[1024,768]{1,0:T(8,128)(2,1)} %tok_ref.5, f32[1024,768]{1,0:T(8,128)} %get-tuple-element.184.grad_ref, f32[1,768]{1,0:T(1,128)} %reshape.1062.gain_ref, bf16[768,1280]{1,0:T(8,128)(2,1)} %bitcast.281, bf16[768,1152]{1,0:T(8,128)(2,1)} %bitcast.283, ...), custom_call_target="tpu_custom_call" | custom-call | flops 517500000 | tf_op jit(solution)/shard_map/token_back/pallas_call | solution.py:643
  401.1 4.7 %collective-permute-done.49 = bf16[1,256,768]{2,1,0:T(8,128)(2,1)} collective-permute-done((bf16[1,256,768]{2,1,0:T(8,128)(2,1)}, bf16[1,256,768]{2,1,0:T(8,128)(2,1)}, u32[]{:S(2)}, u32[]{:S(2)}) %collective-permute-start.49) | collective-permute-done | bytes 393248 | tf_op jit(solution)/shard_map/ppermute | solution.py:663
  417.3 4.6 collective-permute-done.39
  430.4 7.9 %collective-permute-done.44 = bf16[2,48,1536]{2,1,0:T(8,128)(2,1)S(1)} collective-permute-done((bf16[2,48,1536]{2,1,0:T(8,128)(2,1)S(1)}, bf16[2,48,1536]{2,1,0:T(8,128)(2,1)S(1)}, u32[]{:S(2)}, u32[]{:S(2)}) %collective-permute-start.44) | collective-permute-done | bytes 294944 | tf_op jit(solution)/shard_map/ppermute | solution.py:663
  440.2 8.1 %collective-permute-done.45 = bf16[1,48,1536]{2,1,0:T(8,128)(2,1)S(1)} collective-permute-done((bf16[1,48,1536]{2,1,0:T(8,128)(2,1)S(1)}, bf16[1,48,1536]{2,1,0:T(8,128)(2,1)S(1)}, u32[]{:S(2)}, u32[]{:S(2)}) %collective-permute-start.45) | collective-permute-done | bytes 147488 | tf_op jit(solution)/shard_map/ppermute | solution.py:663
  (334 shorter events, 177.3 us)
Async XLA Ops:
  2.7 25.0 %collective-permute-start = (bf16[48,1280]{1,0:T(8,128)(2,1)S(1)}, bf16[48,1280]{1,0:T(8,128)(2,1)S(1)}, u32[]{:S(2)}, u32[]{:S(2)}) collective-permute-start(bf16[48,1280]{1,0:T(8,128)(2,1)S(1)} %dynamic-slice_bitcast_fusion.1), channel_id=1, source_target_pairs={{0,1},{1,2},{2,3},{3,0},{4,5},{5,6},{6,7},{7,4},{8,9},{9,10},{10,1... | collective-permute-start | bytes 368648 | tf_op jit(solution)/shard_map/ppermute | solution.py:784
  4.9 24.2 %collective-permute-start.1 = (bf16[48,1280]{1,0:T(8,128)(2,1)S(1)}, bf16[48,1280]{1,0:T(8,128)(2,1)S(1)}, u32[]{:S(2)}, u32[]{:S(2)}) collective-permute-start(bf16[48,1280]{1,0:T(8,128)(2,1)S(1)} %dynamic-slice_bitcast_fusion.1), channel_id=1, source_target_pairs={{0,2},{1,3},{2,0},{3,1},{4,6},{5,7},{6,4},{7,5},{8,10},{9,11},{10,... | collective-permute-start | bytes 368648 | tf_op jit(solution)/shard_map/ppermute | solution.py:784
  25.7 43.9 %collective-permute-start.15 = (s32[1024]{0:T(1024)S(1)}, s32[1024]{0:T(1024)S(1)}, u32[]{:S(2)}, u32[]{:S(2)}) collective-permute-start(s32[1024]{0:T(1024)S(1)} %bitcast.343), channel_id=1, source_target_pairs={{0,4},{4,0},{1,5},{5,1},{2,6},{6,2},{3,7},{7,3},{8,12},{12,8},{9,1... | collective-permute-start | bytes 12296 | tf_op jit(solution)/shard_map/ppermute | solution.py:663
  27.0 128.1 %collective-permute-start.17 = (bf16[1024,768]{1,0:T(8,128)(2,1)}, bf16[1024,768]{1,0:T(8,128)(2,1)}, u32[]{:S(2)}, u32[]{:S(2)}) collective-permute-start(bf16[1024,768]{1,0:T(8,128)(2,1)} %cot_ref.3), channel_id=1, source_target_pairs={{0,4},{4,0},{1,5},{5,1},{2,6},{6,2},{3,7},{7,3},{8,12},{12,8},{9,1... | collective-permute-start | bytes 4718600 | tf_op jit(solution)/shard_map/ppermute | solution.py:663
  76.0 25.8 %collective-permute-start.14 = (bf16[4,2,48,1024]{3,2,1,0:T(8,128)(2,1)S(1)}, bf16[4,2,48,1024]{3,2,1,0:T(8,128)(2,1)}, u32[]{:S(2)}, u32[]{:S(2)}) collective-permute-start(bf16[4,2,48,1024]{3,2,1,0:T(8,128)(2,1)S(1)} %maximum_bitcast_fusion.2), channel_id=1, source_target_pairs={{0,8},{8,0},{16,24},{24,16},{1,9},{9,1},{17,25},{25,17},{2,10},{10... | collective-permute-start | bytes 2359304 | tf_op jit(solution)/shard_map/ppermute | solution.py:663
  110.2 44.9 %collective-permute-start.16 = (bf16[1024,768]{1,0:T(8,128)(2,1)}, bf16[1024,768]{1,0:T(8,128)(2,1)S(1)}, u32[]{:S(2)}, u32[]{:S(2)}) collective-permute-start(bf16[1024,768]{1,0:T(8,128)(2,1)} %get-tuple-element.111.rows_ref.second_ref), channel_id=1, source_target_pairs={{0,4},{4,0},{1,5},{5,1},{2,6},{6,2},{3,7},{7,3},{8,12},{12,8},{9,1... | collective-permute-start | bytes 4718600 | tf_op jit(solution)/shard_map/ppermute | solution.py:663
  224.2 28.8 %collective-permute-start.24 = (bf16[4,512,768]{2,1,0:T(8,128)(2,1)}, bf16[4,512,768]{2,1,0:T(8,128)(2,1)}, u32[]{:S(2)}, u32[]{:S(2)}) collective-permute-start(bf16[4,512,768]{2,1,0:T(8,128)(2,1)} %get-tuple-element.147), channel_id=1, source_target_pairs={{0,8},{8,0},{16,24},{24,16},{1,9},{9,1},{17,25},{25,17},{2,10},{10... | collective-permute-start | bytes 9437192 | tf_op jit(solution)/shard_map/ppermute | solution.py:663
  224.8 28.2 %collective-permute-start.25 = (bf16[4,256,768]{2,1,0:T(8,128)(2,1)}, bf16[4,256,768]{2,1,0:T(8,128)(2,1)}, u32[]{:S(2)}, u32[]{:S(2)}) collective-permute-start(bf16[4,256,768]{2,1,0:T(8,128)(2,1)} %get-tuple-element.148), channel_id=1, source_target_pairs={{0,8},{8,0},{16,24},{24,16},{1,9},{9,1},{17,25},{25,17},{2,10},{10... | collective-permute-start | bytes 4718600 | tf_op jit(solution)/shard_map/ppermute | solution.py:663
  227.8 40.2 %collective-permute-start.26 = (bf16[4,256,768]{2,1,0:T(8,128)(2,1)}, bf16[4,256,768]{2,1,0:T(8,128)(2,1)}, u32[]{:S(2)}, u32[]{:S(2)}) collective-permute-start(bf16[4,256,768]{2,1,0:T(8,128)(2,1)} %fusion), channel_id=1, source_target_pairs={{0,16},{8,24},{16,0},{24,8},{1,17},{9,25},{17,1},{25,9},{2,18},{10... | collective-permute-start | bytes 4718600 | tf_op jit(solution)/shard_map/ppermute | solution.py:663
  270.8 38.5 %collective-permute-start.28 = (bf16[2,256,768]{2,1,0:T(8,128)(2,1)}, bf16[2,256,768]{2,1,0:T(8,128)(2,1)}, u32[]{:S(2)}, u32[]{:S(2)}) collective-permute-start(bf16[2,256,768]{2,1,0:T(8,128)(2,1)} %fusion.4), channel_id=1, source_target_pairs={{0,1},{1,0},{2,3},{3,2},{4,5},{5,4},{6,7},{7,6},{8,9},{9,8},{10,11... | collective-permute-start | bytes 2359304 | tf_op jit(solution)/shard_map/ppermute | solution.py:663
  273.6 35.6 %collective-permute-start.29 = (bf16[1,256,768]{2,1,0:T(8,128)(2,1)}, bf16[1,256,768]{2,1,0:T(8,128)(2,1)}, u32[]{:S(2)}, u32[]{:S(2)}) collective-permute-start(bf16[1,256,768]{2,1,0:T(8,128)(2,1)} %fusion.18), channel_id=1, source_target_pairs={{0,2},{1,3},{2,0},{3,1},{4,6},{5,7},{6,4},{7,5},{8,10},{9,11},{10,... | collective-permute-start | bytes 1179656 | tf_op jit(solution)/shard_map/ppermute | solution.py:663
  277.7 36.5 %collective-permute-start.30 = (bf16[2,256,768]{2,1,0:T(8,128)(2,1)}, bf16[2,256,768]{2,1,0:T(8,128)(2,1)}, u32[]{:S(2)}, u32[]{:S(2)}) collective-permute-start(bf16[2,256,768]{2,1,0:T(8,128)(2,1)} %fusion.5), channel_id=1, source_target_pairs={{0,1},{1,0},{2,3},{3,2},{4,5},{5,4},{6,7},{7,6},{8,9},{9,8},{10,11... | collective-permute-start | bytes 2359304 | tf_op jit(solution)/shard_map/ppermute | solution.py:663
  281.1 59.8 %collective-permute-start.31 = (bf16[4,256,768]{2,1,0:T(8,128)(2,1)}, bf16[4,256,768]{2,1,0:T(8,128)(2,1)}, u32[]{:S(2)}, u32[]{:S(2)}) collective-permute-start(bf16[4,256,768]{2,1,0:T(8,128)(2,1)} %fusion.1), channel_id=1, source_target_pairs={{0,16},{8,24},{16,0},{24,8},{1,17},{9,25},{17,1},{25,9},{2,18},{10... | collective-permute-start | bytes 4718600 | tf_op jit(solution)/shard_map/ppermute | solution.py:663
  302.7 38.2 %collective-permute-start.32 = (bf16[4,96,1792]{2,1,0:T(8,128)(2,1)}, bf16[4,96,1792]{2,1,0:T(8,128)(2,1)}, u32[]{:S(2)}, u32[]{:S(2)}) collective-permute-start(bf16[4,96,1792]{2,1,0:T(8,128)(2,1)} %pad_maximum_fusion.5), channel_id=1, source_target_pairs={{0,8},{8,0},{16,24},{24,16},{1,9},{9,1},{17,25},{25,17},{2,10},{10... | collective-permute-start | bytes 4128776 | tf_op jit(solution)/shard_map/ppermute | solution.py:663
  309.2 56.1 %collective-permute-start.27 = (bf16[1024,768]{1,0:T(8,128)(2,1)}, bf16[1024,768]{1,0:T(8,128)(2,1)}, u32[]{:S(2)}, u32[]{:S(2)}) collective-permute-start(bf16[1024,768]{1,0:T(8,128)(2,1)} %get-tuple-element.157), channel_id=1, source_target_pairs={{0,4},{4,0},{1,5},{5,1},{2,6},{6,2},{3,7},{7,3},{8,12},{12,8},{9,1... | collective-permute-start | bytes 4718600 | tf_op jit(solution)/shard_map/ppermute | solution.py:663
  319.0 55.4 %collective-permute-start.34 = (bf16[1,256,768]{2,1,0:T(8,128)(2,1)}, bf16[1,256,768]{2,1,0:T(8,128)(2,1)}, u32[]{:S(2)}, u32[]{:S(2)}) collective-permute-start(bf16[1,256,768]{2,1,0:T(8,128)(2,1)} %fusion.17), channel_id=1, source_target_pairs={{0,2},{1,3},{2,0},{3,1},{4,6},{5,7},{6,4},{7,5},{8,10},{9,11},{10,... | collective-permute-start | bytes 1179656 | tf_op jit(solution)/shard_map/ppermute | solution.py:663
  338.4 36.0 %collective-permute-start.35 = (bf16[1,256,768]{2,1,0:T(8,128)(2,1)}, bf16[1,256,768]{2,1,0:T(8,128)(2,1)}, u32[]{:S(2)}, u32[]{:S(2)}) collective-permute-start(bf16[1,256,768]{2,1,0:T(8,128)(2,1)} %fusion.16), channel_id=1, source_target_pairs={{0,2},{1,3},{2,0},{3,1},{4,6},{5,7},{6,4},{7,5},{8,10},{9,11},{10,... | collective-permute-start | bytes 1179656 | tf_op jit(solution)/shard_map/ppermute | solution.py:663
  343.5 31.0 %collective-permute-start.33 = (bf16[2,256,768]{2,1,0:T(8,128)(2,1)}, bf16[2,256,768]{2,1,0:T(8,128)(2,1)}, u32[]{:S(2)}, u32[]{:S(2)}) collective-permute-start(bf16[2,256,768]{2,1,0:T(8,128)(2,1)} %fusion.6), channel_id=1, source_target_pairs={{0,1},{1,0},{2,3},{3,2},{4,5},{5,4},{6,7},{7,6},{8,9},{9,8},{10,11... | collective-permute-start | bytes 2359304 | tf_op jit(solution)/shard_map/ppermute | solution.py:663
  346.3 28.2 %collective-permute-start.36 = (bf16[4,48,1792]{2,1,0:T(8,128)(2,1)}, bf16[4,48,1792]{2,1,0:T(8,128)(2,1)}, u32[]{:S(2)}, u32[]{:S(2)}) collective-permute-start(bf16[4,48,1792]{2,1,0:T(8,128)(2,1)} %fusion.24), channel_id=1, source_target_pairs={{0,4},{4,0},{1,5},{5,1},{2,6},{6,2},{3,7},{7,3},{8,12},{12,8},{9,1... | collective-permute-start | bytes 2064392 | tf_op jit(solution)/shard_map/ppermute | solution.py:663
  365.3 33.1 %collective-permute-start.42 = (bf16[4,96,1536]{2,1,0:T(8,128)(2,1)}, bf16[4,96,1536]{2,1,0:T(8,128)(2,1)}, u32[]{:S(2)}, u32[]{:S(2)}) collective-permute-start(bf16[4,96,1536]{2,1,0:T(8,128)(2,1)} %pad_maximum_fusion.8), channel_id=1, source_target_pairs={{0,8},{8,0},{16,24},{24,16},{1,9},{9,1},{17,25},{25,17},{2,10},{10... | collective-permute-start | bytes 3538952 | tf_op jit(solution)/shard_map/ppermute | solution.py:663
  379.9 33.4 %collective-permute-start.51 = (bf16[256,768]{1,0:T(8,128)(2,1)}, bf16[256,768]{1,0:T(8,128)(2,1)}, u32[]{:S(2)}, u32[]{:S(2)}) collective-permute-start(bf16[256,768]{1,0:T(8,128)(2,1)} %fusion.33), channel_id=1, source_target_pairs={{0,16},{8,24},{16,0},{24,8},{1,17},{9,25},{17,1},{25,9},{2,18},{10... | collective-permute-start | bytes 1179656 | tf_op jit(solution)/shard_map/ppermute | solution.py:663
  399.8 30.3 %collective-permute-start.43 = (bf16[4,48,1536]{2,1,0:T(8,128)(2,1)S(1)}, bf16[4,48,1536]{2,1,0:T(8,128)(2,1)S(1)}, u32[]{:S(2)}, u32[]{:S(2)}) collective-permute-start(bf16[4,48,1536]{2,1,0:T(8,128)(2,1)S(1)} %fusion.25), channel_id=1, source_target_pairs={{0,4},{4,0},{1,5},{5,1},{2,6},{6,2},{3,7},{7,3},{8,12},{12,8},{9,1... | collective-permute-start | bytes 1769480 | tf_op jit(solution)/shard_map/ppermute | solution.py:663
  410.6 44.1 %collective-permute-start.55 = (bf16[768,768]{1,0:T(8,128)(2,1)}, bf16[768,768]{1,0:T(8,128)(2,1)}, u32[]{:S(2)}, u32[]{:S(2)}) collective-permute-start(bf16[768,768]{1,0:T(8,128)(2,1)} %pad_maximum_fusion.10), channel_id=1, source_target_pairs={{0,8},{8,0},{16,24},{24,16},{1,9},{9,1},{17,25},{25,17},{2,10},{10... | collective-permute-start | bytes 3538952 | tf_op jit(solution)/shard_map/ppermute | solution.py:663
  430.1 30.8 %collective-permute-start.52 = (bf16[768,768]{1,0:T(8,128)(2,1)}, bf16[768,768]{1,0:T(8,128)(2,1)}, u32[]{:S(2)}, u32[]{:S(2)}) collective-permute-start(bf16[768,768]{1,0:T(8,128)(2,1)} %pad_maximum_fusion.9), channel_id=1, source_target_pairs={{0,8},{8,0},{16,24},{24,16},{1,9},{9,1},{17,25},{25,17},{2,10},{10... | collective-permute-start | bytes 3538952 | tf_op jit(solution)/shard_map/ppermute | solution.py:663
  (73 other events, 901.6 us)
